TPU v7x, 128 devices: a whole 4x4x4 slice. The times are simulated.
128 devices in a mesh: gx: 32 (over z_hi, x, y), yz: 4 (over z_lo, core).
Axes of the slice: x: 4, y: 4, z: 4 (z_hi: 2, z_lo: 2; z = z_hi * 2 + z_lo), core: 2. Of those that a mesh axis runs over, the one named last changes fastest.
Arguments:
- positions: float32 [3, 6144], P(None, ('gx', 'yz')), may hold values from -6 to 6
- velocities: float32 [3, 6144], P(None, ('gx', 'yz')), may hold values from -6 to 6
- forces_start: float32 [3, 6144], P(None, ('gx', 'yz')), may hold values from -6 to 6
- species: int32 [6144], P(('gx', 'yz')), may hold values from 0 to 7
- live_atoms: int32 [128], P(('gx', 'yz')), may hold values from 12 to 48, as said below
- send_list: int32 [8, 1536], P(None, ('gx', 'yz')), may hold values from 0 to 47, as said below
- neighbours: int32 [6144, 128], P(('gx', 'yz')), may hold values from 0 to 143, as said below
- neighbour_count: int32 [6144], P(('gx', 'yz')), may hold values from 64 to 128
- radial_weight: bfloat16 [8, 512], replicated, may hold values from -4 to 4
- species_embed: bfloat16 [2, 8, 512], replicated, may hold values from -2 to 2
- env_weight: bfloat16 [1, 512, 64], replicated, may hold values from -0.25 to 0.25
- latent_weight: bfloat16 [1, 576, 512], replicated, may hold values from -0.25 to 0.25
- readout: bfloat16 [512], replicated, may hold values from -0.0625 to 0.0625
Outputs:
- positions_end: float32 [3, 6144], P(None, ('gx', 'yz'))
- velocities_end: float32 [3, 6144], P(None, ('gx', 'yz'))
- forces_end: float32 [3, 6144], P(None, ('gx', 'yz'))
Inputs may be any that keep to these rules, and one draw needn't show every extreme that they name: `live_atoms`: atoms in use are the first ones of a domain's slots; some domain uses all 48 in every draw. `send_list`: each row names distinct atoms in use of the sending domain. `neighbours`: each entry names an own atom in use or a ghost slot.
All inputs are finite; a program needn't handle non-finite values.
Results may differ from a plain program's by a relative error of at most 0.038.
Values sent between devices are 32-bit elements; how exact they have to be, the bound alone decides.
A program may use at most 64 MiB of HBM per device.

v0:
```python
import jax
import jax.numpy as jnp
from jax import lax
from jax.sharding import PartitionSpec as P

SPECIES = 8
CENTRES = 4


RADIUS = 6.0
STEP = 0.25
COUPLING = 4.0
MASSES = (1.008, 12.011, 14.007, 15.999, 32.06, 22.99, 35.45, 30.97)


def padded(cells, sides, width):
    for axis, dim in sides:
        count = lax.axis_size(axis)
        head = lax.slice_in_dim(cells, 0, width, axis=dim)
        tail = lax.slice_in_dim(cells, cells.shape[dim] - width, cells.shape[dim], axis=dim)
        cells = jnp.concatenate(
            [
                lax.ppermute(tail, axis, [(i, (i + 1) % count) for i in range(count)]),
                cells,
                lax.ppermute(head, axis, [((i + 1) % count, i) for i in range(count)]),
            ],
            axis=dim,
        )
    return cells


def inverse_mass(species):
    inv_total = jnp.zeros(species.shape, jnp.float32)
    for spec_id in range(len(MASSES)):
        inv_total = inv_total + jnp.where(
            species == spec_id, jnp.float32(1.0 / MASSES[spec_id]), jnp.float32(0.0)
        )
    return inv_total


def pick_columns(values, select):
    return lax.dot_general(
        values,
        select,
        (((1,), (1,)), ((), ())),
        precision=lax.Precision.HIGHEST,
        preferred_element_type=jnp.float32,
    )


def block_energy(
    centre_pos,
    neigh_pos,
    centre_kind,
    neigh_kind,
    pair_mask,
    radial_weight,
    species_embed,
    env_weight,
    latent_weight,
    readout,
):
    count_c = centre_pos.shape[1]
    slot_n = neigh_pos.shape[2]
    row_count = count_c * slot_n
    scaled = (neigh_pos - centre_pos[:, :, None]) * (1.0 / RADIUS)
    vectors = scaled.reshape(3, row_count)
    square = jnp.sum(vectors * vectors, axis=0)
    envelope = jnp.square(jnp.maximum(1.0 - square, 0.0)) * pair_mask.reshape(row_count)
    basis_n = radial_weight.shape[0]
    basis_mid = (jnp.arange(basis_n, dtype=jnp.float32) + 0.5) / basis_n
    basis_vals = jnp.exp(
        -2.0 * basis_n * basis_n * jnp.square(square[:, None] - basis_mid[None, :])
    )
    centre_embed = jnp.dot(centre_kind, species_embed[0], preferred_element_type=jnp.float32)
    feat_width = centre_embed.shape[1]
    preact = jnp.dot(
        basis_vals.astype(jnp.bfloat16), radial_weight, preferred_element_type=jnp.float32
    )
    preact = preact + jnp.dot(neigh_kind, species_embed[1], preferred_element_type=jnp.float32)
    preact = (preact.reshape(count_c, slot_n, feat_width) + centre_embed[:, None, :]).reshape(
        row_count, feat_width
    )
    hidden = jax.nn.silu(preact)
    norm_scale = slot_n ** (-0.5)
    weights = (
        jnp.dot(hidden.astype(jnp.bfloat16), env_weight[0], preferred_element_type=jnp.float32)
        * envelope[:, None]
    )
    tensor = vectors[:, :, None] * weights[None, :, :]
    grouped = tensor.reshape(3, count_c, slot_n, weights.shape[1])
    centre_tensor = jnp.sum(grouped, axis=2) * norm_scale
    inner_prod = COUPLING * jnp.sum(grouped * centre_tensor[:, :, None, :], axis=0).reshape(
        row_count, weights.shape[1]
    )
    joined = jnp.concatenate([hidden, inner_prod], axis=1).astype(jnp.bfloat16)
    hidden = hidden + jax.nn.silu(
        jnp.dot(joined, latent_weight[0], preferred_element_type=jnp.float32)
    )
    pair_energy = jnp.dot(hidden.astype(jnp.bfloat16), readout, preferred_element_type=jnp.float32)
    return jnp.sum(pair_energy * envelope)


def block_update(forces, block_id, ext_pos, ext_kinds, neighbours, counts, live_count, params):
    first = (block_id * CENTRES).astype(jnp.int32)
    ext_n = ext_pos.shape[1]
    slot_n = neighbours.shape[1]
    centre_pos = lax.dynamic_slice_in_dim(ext_pos, first, CENTRES, 1)
    neigh_idx = lax.dynamic_slice_in_dim(neighbours, first, CENTRES, 0)
    selected = neigh_idx.reshape(-1)[:, None] == jnp.arange(ext_n, dtype=jnp.int32)[None, :]
    select_float = selected.astype(jnp.float32)
    neigh_pos = pick_columns(ext_pos, select_float).reshape(3, CENTRES, slot_n)
    centre_kind = lax.dynamic_slice_in_dim(ext_kinds, first, CENTRES, 0)
    neigh_kind = jnp.dot(
        selected.astype(jnp.bfloat16), ext_kinds, preferred_element_type=jnp.float32
    ).astype(jnp.bfloat16)
    block_counts = lax.dynamic_slice_in_dim(counts, first, CENTRES, 0)
    alive_rows = first + jnp.arange(CENTRES, dtype=jnp.int32) < live_count
    in_use = (jnp.arange(slot_n, dtype=jnp.int32)[None, :] < block_counts[:, None]) & alive_rows[
        :, None
    ]
    pair_mask = jnp.where(in_use, jnp.float32(1.0), jnp.float32(0.0))

    def energy_of(centre_arg, neigh_arg):
        return block_energy(centre_arg, neigh_arg, centre_kind, neigh_kind, pair_mask, *params)

    energy, pullback = jax.vjp(energy_of, centre_pos, neigh_pos)
    grad_c, grad_n = pullback(jnp.ones_like(energy))
    current = lax.dynamic_slice_in_dim(forces, first, CENTRES, 1)
    forces = lax.dynamic_update_slice_in_dim(forces, current - grad_c, first, 1)
    spread = jnp.dot(
        -grad_n.reshape(3, -1),
        select_float,
        precision=lax.Precision.HIGHEST,
        preferred_element_type=jnp.float32,
    )
    return forces + spread


def forward_gx_first(payload):
    ghost_len = payload.shape[2]
    packed = jnp.stack([payload[0:3], payload[5:8]]).reshape(2, -1)
    spread = padded(packed, (("gx", 0),), 1).reshape(4, 3, 4, ghost_len)
    from_low = spread[0]
    from_high = spread[3]
    packed = jnp.stack(
        [
            jnp.stack([from_high[0], payload[3], from_low[0]]),
            jnp.stack([from_high[2], payload[4], from_low[2]]),
        ]
    ).reshape(2, -1)
    spread = padded(packed, (("yz", 0),), 1).reshape(4, 3, 4, ghost_len)
    from_below = spread[0]
    from_above = spread[3]
    return jnp.stack(
        [
            from_above[0],
            from_high[1],
            from_below[0],
            from_above[1],
            from_below[1],
            from_above[2],
            from_low[1],
            from_below[2],
        ]
    )


def return_gx_first(ghost_force):
    ghost_len = ghost_force.shape[2]
    packed = jnp.stack(
        [
            jnp.stack([ghost_force[2], ghost_force[4], ghost_force[7]]),
            jnp.stack([ghost_force[0], ghost_force[3], ghost_force[5]]),
        ]
    ).reshape(2, -1)
    spread = padded(packed, (("yz", 0),), 1).reshape(4, 3, 3, ghost_len)
    from_below = spread[0]
    from_above = spread[3]
    packed = jnp.stack(
        [
            jnp.stack([from_below[2], ghost_force[6], from_above[2]]),
            jnp.stack([from_below[0], ghost_force[1], from_above[0]]),
        ]
    ).reshape(2, -1)
    spread = padded(packed, (("gx", 0),), 1).reshape(4, 3, 3, ghost_len)
    from_low = spread[0]
    from_high = spread[3]
    return jnp.stack(
        [
            from_low[0],
            from_low[1],
            from_low[2],
            from_below[1],
            from_above[1],
            from_high[0],
            from_high[1],
            from_high[2],
        ]
    )


def body(
    positions,
    velocities,
    forces_start,
    species,
    live_atoms,
    send_list,
    neighbours,
    neighbour_count,
    radial_weight,
    species_embed,
    env_weight,
    latent_weight,
    readout,
):
    atom_n = positions.shape[1]
    ghost_len = send_list.shape[1]
    live_count = live_atoms[0]
    species_float = species.astype(jnp.float32)
    inverse = inverse_mass(species)
    params = (radial_weight, species_embed, env_weight, latent_weight, readout)
    kind_ids = jnp.arange(SPECIES, dtype=jnp.float32)
    send_pick = (
        send_list.reshape(-1)[:, None] == jnp.arange(atom_n, dtype=jnp.int32)[None, :]
    ).astype(jnp.float32)

    def evaluate(coords):
        sources = jnp.concatenate([coords, species_float[None]], axis=0)
        payload = pick_columns(sources, send_pick).reshape(4, 8, ghost_len).transpose(1, 0, 2)
        ghosts = forward_gx_first(payload)
        ext_pos = jnp.concatenate(
            [coords, ghosts[:, 0:3].transpose(1, 0, 2).reshape(3, -1)], axis=1
        )
        ext_species = jnp.concatenate([species_float, ghosts[:, 3].reshape(-1)])
        ext_kinds = (ext_species[:, None] == kind_ids[None, :]).astype(jnp.bfloat16)

        def one_block(block_id, forces):
            return block_update(
                forces,
                block_id,
                ext_pos,
                ext_kinds,
                neighbours,
                neighbour_count,
                live_count,
                params,
            )

        rounds = atom_n // CENTRES
        forces = lax.fori_loop(0, rounds, one_block, jnp.zeros((3, ext_pos.shape[1]), jnp.float32))
        ghost_force = forces[:, atom_n:].reshape(3, 8, -1).transpose(1, 0, 2)
        returned = return_gx_first(ghost_force)
        back = jnp.dot(
            returned.transpose(1, 0, 2).reshape(3, -1),
            send_pick,
            precision=lax.Precision.HIGHEST,
            preferred_element_type=jnp.float32,
        )
        return forces[:, :atom_n] + back

    half = velocities + 0.5 * STEP * inverse * forces_start
    moved = positions + STEP * half
    forces_mid = evaluate(moved)
    velocities_mid = half + 0.5 * STEP * inverse * forces_mid
    half_two = velocities_mid + 0.5 * STEP * inverse * forces_mid
    positions_end = moved + STEP * half_two
    forces_end = evaluate(positions_end)
    velocities_end = half_two + 0.5 * STEP * inverse * forces_end
    return (positions_end, velocities_end, forces_end)


def solution(mesh):
    placed = (
        P(None, ("gx", "yz")),
        P(None, ("gx", "yz")),
        P(None, ("gx", "yz")),
        P(("gx", "yz")),
        P(("gx", "yz")),
        P(None, ("gx", "yz")),
        P(("gx", "yz"), None),
        P(("gx", "yz")),
        P(),
        P(),
        P(),
        P(),
        P(),
    )
    return jax.shard_map(
        body,
        mesh=mesh,
        in_specs=placed,
        out_specs=(P(None, ("gx", "yz")), P(None, ("gx", "yz")), P(None, ("gx", "yz"))),
        check_vma=False,
    )
```

profile of v0, /device:TPU:1, one launch (start us, length us, event | category | flops | bytes accessed | tf_op | source)
XLA Modules:
  0.0 393.7 jit_solution(10417832185456268906)
XLA Ops:
  3.9 2.2 collective-permute-start.1
  6.2 7.0 %collective-permute-start = (f32[1,144]{1,0:T(1,128)S(1)}, f32[1,144]{1,0:T(1,128)S(1)}, u32[]{:S(2)}, u32[]{:S(2)}) collective-permute-start(f32[1,144]{1,0:T(1,128)S(1)} %slice.509), channel_id=1, source_target_pairs={{4,0},{8,4},{12,8},{16,12},{20,16},{24,20},{28,24},{32,28},{36,32}... | collective-permute-start | bytes 1736 | tf_op jit(solution)/shard_map/ppermute | solution.py:25
  19.4 164.7 %while.28 = (s32[]{:T(128)}, f32[3,144]{1,0:T(4,128)S(1)}, s32[48,128]{1,0:T(8,128)}, f32[3,144]{1,0:T(4,128)S(1)}, s32[48]{0:T(128)}, /*index=5*/s32[]{:T(128)}...) while((s32[]{:T(128)}, f32[3,144]{1,0:T(4,128)S(1)}, ...), condition=%wide.region_10.11_spmd.clone, body=%wide.region_0.10_spmd.clone.sunk | while | flops 706163584 | bytes 29330392 | solution.py:252
  25.6 1.7 fusion.305
  39.2 1.7 fusion.305
  52.9 1.7 fusion.305
  66.7 1.7 fusion.305
  80.4 1.7 fusion.305
  94.1 1.7 fusion.305
  107.9 1.7 fusion.305
  121.6 1.7 fusion.305
  135.3 1.7 fusion.305
  149.1 1.7 fusion.305
  162.8 1.7 fusion.305
  176.5 1.7 fusion.305
  184.3 1.7 collective-permute-start.4
  187.0 2.1 collective-permute-done.5
  189.8 8.0 %collective-permute-start.7 = (f32[1,108]{1,0:T(1,128)S(1)}, f32[1,108]{1,0:T(1,128)S(1)}, u32[]{:S(2)}, u32[]{:S(2)}) collective-permute-start(f32[1,108]{1,0:T(1,128)S(1)} %slice.573), channel_id=1, source_target_pairs={{4,0},{8,4},{12,8},{16,12},{20,16},{24,20},{28,24},{32,28},{36,32}... | collective-permute-start | bytes 1304 | tf_op jit(solution)/shard_map/ppermute | solution.py:25
  200.1 7.2 %collective-permute-start.8 = (f32[1,144]{1,0:T(1,128)S(1)}, f32[1,144]{1,0:T(1,128)S(1)}, u32[]{:S(2)}, u32[]{:S(2)}) collective-permute-start(f32[1,144]{1,0:T(1,128)S(1)} %slice.581), channel_id=1, source_target_pairs={{4,0},{8,4},{12,8},{16,12},{20,16},{24,20},{28,24},{32,28},{36,32}... | collective-permute-start | bytes 1736 | tf_op jit(solution)/shard_map/ppermute | solution.py:25
  213.0 164.5 %while.29 = (s32[]{:T(128)}, f32[3,144]{1,0:T(4,128)S(1)}, s32[48,128]{1,0:T(8,128)}, f32[3,144]{1,0:T(4,128)S(1)}, s32[48]{0:T(128)}, /*index=5*/s32[]{:T(128)}...) while((s32[]{:T(128)}, f32[3,144]{1,0:T(4,128)S(1)}, ...), condition=%wide.region_21.22_spmd.clone, body=%wide.region_11.21_spmd.clone.sunk | while | flops 706163584 | bytes 25136060 | solution.py:252
  219.2 1.7 fusion.340
  232.8 1.7 fusion.340
  246.5 1.7 fusion.340
  260.2 1.7 fusion.340
  273.9 1.7 fusion.340
  301.4 1.7 fusion.340
  315.1 1.7 fusion.340
  342.5 1.7 fusion.340
  356.3 1.7 fusion.340
  377.8 1.9 collective-permute-start.12
  380.7 2.1 collective-permute-done.13
  383.4 8.0 %collective-permute-start.15 = (f32[1,108]{1,0:T(1,128)S(1)}, f32[1,108]{1,0:T(1,128)S(1)}, u32[]{:S(2)}, u32[]{:S(2)}) collective-permute-start(f32[1,108]{1,0:T(1,128)S(1)} %slice.645), channel_id=1, source_target_pairs={{4,0},{8,4},{12,8},{16,12},{20,16},{24,20},{28,24},{32,28},{36,32}... | collective-permute-start | bytes 1304 | tf_op jit(solution)/shard_map/ppermute | solution.py:25
  (1383 shorter events, 313.4 us)
Async XLA Ops:
  3.9 10.1 %collective-permute-start.1 = (f32[1,144]{1,0:T(1,128)S(1)}, f32[1,144]{1,0:T(1,128)S(1)}, u32[]{:S(2)}, u32[]{:S(2)}) collective-permute-start(f32[1,144]{1,0:T(1,128)S(1)} %slice.514), channel_id=1, source_target_pairs={{0,4},{4,8},{8,12},{12,16},{16,20},{20,24},{24,28},{28,32},{32,36}... | collective-permute-start | bytes 1736 | tf_op jit(solution)/shard_map/ppermute | solution.py:23
  6.2 8.1 %collective-permute-start = (f32[1,144]{1,0:T(1,128)S(1)}, f32[1,144]{1,0:T(1,128)S(1)}, u32[]{:S(2)}, u32[]{:S(2)}) collective-permute-start(f32[1,144]{1,0:T(1,128)S(1)} %slice.509), channel_id=1, source_target_pairs={{4,0},{8,4},{12,8},{16,12},{20,16},{24,20},{28,24},{32,28},{36,32}... | collective-permute-start | bytes 1736 | tf_op jit(solution)/shard_map/ppermute | solution.py:25
  14.6 3.6 collective-permute-start.2
  16.5 2.1 collective-permute-start.3
  19.3 179.9 %copy-start.6 = (f32[3,48]{1,0:T(4,128)S(1)}, f32[3,48]{1,0:T(4,128)}, u32[]{:S(2)}) copy-start(f32[3,48]{1,0:T(4,128)} %param.18) | copy-start | bytes 1732
  19.3 179.9 %copy-start.7 = (f32[3,48]{1,0:T(4,128)S(1)}, f32[3,48]{1,0:T(4,128)}, u32[]{:S(2)}) copy-start(f32[3,48]{1,0:T(4,128)} %param.19) | copy-start | bytes 1732
  33.0 5.9 %copy-start.2 = (bf16[8,512]{1,0:T(8,128)(2,1)S(1)}, bf16[8,512]{1,0:T(8,128)(2,1)}, u32[]{:S(2)}) copy-start(bf16[8,512]{1,0:T(8,128)(2,1)} %get-tuple-element.841) | copy-start | bytes 24580 | tf_op jit(solution)/shard_map/while
  60.4 5.9 %copy-start.2 = (bf16[8,512]{1,0:T(8,128)(2,1)S(1)}, bf16[8,512]{1,0:T(8,128)(2,1)}, u32[]{:S(2)}) copy-start(bf16[8,512]{1,0:T(8,128)(2,1)} %get-tuple-element.841) | copy-start | bytes 24580 | tf_op jit(solution)/shard_map/while
  74.2 5.9 %copy-start.2 = (bf16[8,512]{1,0:T(8,128)(2,1)S(1)}, bf16[8,512]{1,0:T(8,128)(2,1)}, u32[]{:S(2)}) copy-start(bf16[8,512]{1,0:T(8,128)(2,1)} %get-tuple-element.841) | copy-start | bytes 24580 | tf_op jit(solution)/shard_map/while
  87.9 5.9 %copy-start.2 = (bf16[8,512]{1,0:T(8,128)(2,1)S(1)}, bf16[8,512]{1,0:T(8,128)(2,1)}, u32[]{:S(2)}) copy-start(bf16[8,512]{1,0:T(8,128)(2,1)} %get-tuple-element.841) | copy-start | bytes 24580 | tf_op jit(solution)/shard_map/while
  101.6 5.9 %copy-start.2 = (bf16[8,512]{1,0:T(8,128)(2,1)S(1)}, bf16[8,512]{1,0:T(8,128)(2,1)}, u32[]{:S(2)}) copy-start(bf16[8,512]{1,0:T(8,128)(2,1)} %get-tuple-element.841) | copy-start | bytes 24580 | tf_op jit(solution)/shard_map/while
  115.3 5.9 %copy-start.2 = (bf16[8,512]{1,0:T(8,128)(2,1)S(1)}, bf16[8,512]{1,0:T(8,128)(2,1)}, u32[]{:S(2)}) copy-start(bf16[8,512]{1,0:T(8,128)(2,1)} %get-tuple-element.841) | copy-start | bytes 24580 | tf_op jit(solution)/shard_map/while
  129.1 5.9 %copy-start.2 = (bf16[8,512]{1,0:T(8,128)(2,1)S(1)}, bf16[8,512]{1,0:T(8,128)(2,1)}, u32[]{:S(2)}) copy-start(bf16[8,512]{1,0:T(8,128)(2,1)} %get-tuple-element.841) | copy-start | bytes 24580 | tf_op jit(solution)/shard_map/while
  156.5 5.9 %copy-start.2 = (bf16[8,512]{1,0:T(8,128)(2,1)S(1)}, bf16[8,512]{1,0:T(8,128)(2,1)}, u32[]{:S(2)}) copy-start(bf16[8,512]{1,0:T(8,128)(2,1)} %get-tuple-element.841) | copy-start | bytes 24580 | tf_op jit(solution)/shard_map/while
  184.3 2.4 collective-permute-start.4
  186.1 3.0 collective-permute-start.5
  189.5 8.9 %collective-permute-start.6 = (f32[1,108]{1,0:T(1,128)S(1)}, f32[1,108]{1,0:T(1,128)S(1)}, u32[]{:S(2)}, u32[]{:S(2)}) collective-permute-start(f32[1,108]{1,0:T(1,128)S(1)} %slice.557), channel_id=1, source_target_pairs={{0,4},{4,8},{8,12},{12,16},{16,20},{20,24},{24,28},{28,32},{32,36}... | collective-permute-start | bytes 1304 | tf_op jit(solution)/shard_map/ppermute | solution.py:23
  189.8 9.0 %collective-permute-start.7 = (f32[1,108]{1,0:T(1,128)S(1)}, f32[1,108]{1,0:T(1,128)S(1)}, u32[]{:S(2)}, u32[]{:S(2)}) collective-permute-start(f32[1,108]{1,0:T(1,128)S(1)} %slice.573), channel_id=1, source_target_pairs={{4,0},{8,4},{12,8},{16,12},{20,16},{24,20},{28,24},{32,28},{36,32}... | collective-permute-start | bytes 1304 | tf_op jit(solution)/shard_map/ppermute | solution.py:25
  199.5 13.5 %copy-start.8 = (f32[3,48]{1,0:T(4,128)}, f32[3,48]{1,0:T(4,128)S(1)}, u32[]{:S(2)}) copy-start(f32[3,48]{1,0:T(4,128)S(1)} %get-tuple-element.617) | copy-start | bytes 1732
  199.9 8.2 %collective-permute-start.9 = (f32[1,144]{1,0:T(1,128)S(1)}, f32[1,144]{1,0:T(1,128)S(1)}, u32[]{:S(2)}, u32[]{:S(2)}) collective-permute-start(f32[1,144]{1,0:T(1,128)S(1)} %slice.586), channel_id=1, source_target_pairs={{0,4},{4,8},{8,12},{12,16},{16,20},{20,24},{24,28},{28,32},{32,36}... | collective-permute-start | bytes 1736 | tf_op jit(solution)/shard_map/ppermute | solution.py:23
  200.1 8.3 %collective-permute-start.8 = (f32[1,144]{1,0:T(1,128)S(1)}, f32[1,144]{1,0:T(1,128)S(1)}, u32[]{:S(2)}, u32[]{:S(2)}) collective-permute-start(f32[1,144]{1,0:T(1,128)S(1)} %slice.581), channel_id=1, source_target_pairs={{4,0},{8,4},{12,8},{16,12},{20,16},{24,20},{28,24},{32,28},{36,32}... | collective-permute-start | bytes 1736 | tf_op jit(solution)/shard_map/ppermute | solution.py:25
  208.9 3.1 collective-permute-start.10
  209.8 2.1 collective-permute-start.11
  226.5 5.9 %copy-start.3 = (bf16[8,512]{1,0:T(8,128)(2,1)S(1)}, bf16[8,512]{1,0:T(8,128)(2,1)}, u32[]{:S(2)}) copy-start(bf16[8,512]{1,0:T(8,128)(2,1)} %get-tuple-element.895) | copy-start | bytes 24580 | tf_op jit(solution)/shard_map/while
  254.0 5.9 %copy-start.3 = (bf16[8,512]{1,0:T(8,128)(2,1)S(1)}, bf16[8,512]{1,0:T(8,128)(2,1)}, u32[]{:S(2)}) copy-start(bf16[8,512]{1,0:T(8,128)(2,1)} %get-tuple-element.895) | copy-start | bytes 24580 | tf_op jit(solution)/shard_map/while
  295.1 5.9 %copy-start.3 = (bf16[8,512]{1,0:T(8,128)(2,1)S(1)}, bf16[8,512]{1,0:T(8,128)(2,1)}, u32[]{:S(2)}) copy-start(bf16[8,512]{1,0:T(8,128)(2,1)} %get-tuple-element.895) | copy-start | bytes 24580 | tf_op jit(solution)/shard_map/while
  308.9 5.9 %copy-start.3 = (bf16[8,512]{1,0:T(8,128)(2,1)S(1)}, bf16[8,512]{1,0:T(8,128)(2,1)}, u32[]{:S(2)}) copy-start(bf16[8,512]{1,0:T(8,128)(2,1)} %get-tuple-element.895) | copy-start | bytes 24580 | tf_op jit(solution)/shard_map/while
  336.3 5.9 %copy-start.3 = (bf16[8,512]{1,0:T(8,128)(2,1)S(1)}, bf16[8,512]{1,0:T(8,128)(2,1)}, u32[]{:S(2)}) copy-start(bf16[8,512]{1,0:T(8,128)(2,1)} %get-tuple-element.895) | copy-start | bytes 24580 | tf_op jit(solution)/shard_map/while
  377.8 2.6 collective-permute-start.12
  379.8 3.0 collective-permute-start.13
  383.2 8.9 %collective-permute-start.14 = (f32[1,108]{1,0:T(1,128)S(1)}, f32[1,108]{1,0:T(1,128)S(1)}, u32[]{:S(2)}, u32[]{:S(2)}) collective-permute-start(f32[1,108]{1,0:T(1,128)S(1)} %slice.629), channel_id=1, source_target_pairs={{0,4},{4,8},{8,12},{12,16},{16,20},{20,24},{24,28},{28,32},{32,36}... | collective-permute-start | bytes 1304 | tf_op jit(solution)/shard_map/ppermute | solution.py:23
  383.4 8.9 %collective-permute-start.15 = (f32[1,108]{1,0:T(1,128)S(1)}, f32[1,108]{1,0:T(1,128)S(1)}, u32[]{:S(2)}, u32[]{:S(2)}) collective-permute-start(f32[1,108]{1,0:T(1,128)S(1)} %slice.645), channel_id=1, source_target_pairs={{4,0},{8,4},{12,8},{16,12},{20,16},{24,20},{28,24},{32,28},{36,32}... | collective-permute-start | bytes 1304 | tf_op jit(solution)/shard_map/ppermute | solution.py:25
  (119 other events, 198.7 us)
where the time goes:
time: 401 us; the launch traced here: 394 us
  matrix products  162 us (40%)
  local copies, waits for them, and re-layouts  108 us (27%)
  other arithmetic  67.9 us (17%)
  starting transfers between devices  40.5 us (10%)
  waiting for transfers between devices  10.1 us (3%)
    while x312, local copies, waits for them, and re-layouts  43.4 us
    dot_general x24, matrix products, block_energy(): jnp.dot(neigh_kind, species_embed[1], preferred_element_type=jnp.float32)  40.2 us
    ppermute x8, starting transfers between devices, padded(): lax.ppermute(head, axis, [((i + 1) % count, i) for i in range(count)])  32.8 us
    dot_general x48, matrix products, block_energy(): jnp.dot(joined, latent_weight[0], preferred_element_type=jnp.float32)  32.5 us
    dot_general x48, matrix products, block_energy(): jnp.dot(basis_vals.astype(jnp.bfloat16), radial_weight, preferred_element...  26.8 us
    dot_general x24, matrix products, block_energy(): jnp.dot(centre_kind, species_embed[0], preferred_element_type=jnp.float32)  23.2 us
    dynamic_slice x24, local copies, waits for them, and re-layouts, block_update(): block_counts = lax.dynamic_slice_in_dim(counts, first, CENTRES, 0)  17.6 us
    lt x24, other arithmetic, block_update(): alive_rows = first + jnp.arange(CENTRES, dtype=jnp.int32) < live_count  17 us
  transfers between devices with their start and end apart: 16, of which 10 were waited for; matrix products, arithmetic and copies ran while one was open for 1% of the time, Pallas kernels for 0%

commit v1 on v0

v1 whole, which is shorter than its diff:
```python
import functools

import jax
import jax.numpy as jnp
from jax import lax
from jax.experimental import pallas as pl
from jax.experimental.pallas import tpu as pltpu
from jax.sharding import PartitionSpec as P

F32, BF16, I32 = jnp.float32, jnp.bfloat16, jnp.int32
MESH = pl.DeviceIdType.MESH
NT = (((1,), (1,)), ((), ()))

STEP = 0.25
MASSES = (1.008, 12.011, 14.007, 15.999, 32.06, 22.99, 35.45, 30.97)
ATOMS = 48
SLOTS = 128
GHOSTS = 12
N_YZ = 4
EXT = ATOMS + 8 * GHOSTS
NEAR = ATOMS + 2 * GHOSTS
LATENT = 512
FEATURES = 64
SCALE = 4.0 / SLOTS**0.5
CHAINS = 4


def mm(a, b):
    return jnp.dot(a, b, preferred_element_type=F32)


def lanes_of(shape):
    return lax.broadcasted_iota(I32, shape, len(shape) - 1)


def rows_of(shape):
    return lax.broadcasted_iota(I32, shape, 0)


def gather(table, idx):
    return jnp.take_along_axis(table, jnp.broadcast_to(idx, table.shape), axis=1)


def inverse_mass(species):
    total = jnp.zeros(species.shape, F32)
    for kind, mass in enumerate(MASSES):
        total = total + jnp.where(species == kind, jnp.float32(1.0 / mass), jnp.float32(0.0))
    return total


def partners():
    g, q, n = lax.axis_index("gx"), lax.axis_index("yz"), lax.axis_size("gx")
    slab = [(s, g, lax.rem(q + s, N_YZ)) for s in range(1, N_YZ)]
    up, down = lax.rem(g + 1, n), lax.rem(g + n - 1, n)
    above = [(s, up, lax.rem(q + s, N_YZ)) for s in range(N_YZ)]
    below = [(s, down, lax.rem(q + s, N_YZ)) for s in range(N_YZ)]
    return slab, above, below


def greet():
    slab, above, below = partners()
    barrier = pltpu.get_barrier_semaphore()
    for _, g, q in slab + above + below:
        pl.semaphore_signal(barrier, inc=1, device_id=(g, q), device_id_type=MESH)


def greeted():
    pl.semaphore_wait(pltpu.get_barrier_semaphore(), 3 * N_YZ - 1)


def send(src, dst, sems, at, g, q):
    copy = pltpu.make_async_remote_copy(
        src_ref=src,
        dst_ref=dst,
        send_sem=sems.at[0, at],
        recv_sem=sems.at[1, at],
        device_id=(g, q),
        device_id_type=MESH,
    )
    copy.start()
    return copy


def spread(tiles, near, low, high, sems):
    me = lax.axis_index("yz")
    slab, above, below = partners()
    copies = []
    for s, g, q in slab:
        copies.append(send(tiles(q)[0], near.at[me], sems, s - 1, g, q))
    for s, g, q in above:
        copies.append(send(tiles(q)[1], low.at[me], sems, 3 + s, g, q))
    for s, g, q in below:
        copies.append(send(tiles(q)[1], high.at[me], sems, 7 + s, g, q))
    return copies


def assemble(ext_ref, near, low, high):
    lane = lanes_of((8, 128))
    for d in range(N_YZ):
        up, down = (d + 1) % N_YZ, (d - 1) % N_YZ
        ext_ref[d, :, 0:128] = jnp.where(
            lane < ATOMS, near[d], jnp.where(lane < ATOMS + GHOSTS, near[up], near[down])
        )
        hi = jnp.where(lane < 12, high[up], jnp.where(lane < 24, high[d], high[down]))
        lo = jnp.where(lane < 48, low[up], jnp.where(lane < 60, low[d], low[down]))
        ext_ref[d, :, 128:256] = jnp.where(lane < 36, hi, jnp.where(lane < 72, lo, 0.0))


def fold(f_ref, out0, out1):
    lane = lanes_of((8, 128))
    for d in range(N_YZ):
        up, down = (d + 1) % N_YZ, (d - 1) % N_YZ
        out0[d] = jnp.where(
            lane < ATOMS,
            f_ref[d, :, 0:128],
            jnp.where(lane < ATOMS + GHOSTS, f_ref[down, :, 0:128], f_ref[up, :, 0:128]),
        )
        first = (lane < 12) | ((lane >= 36) & (lane < 48))
        second = (lane < 24) | ((lane >= 48) & (lane < 60))
        out1[d] = jnp.where(
            first,
            f_ref[down, :, 128:256],
            jnp.where(second, f_ref[d, :, 128:256], f_ref[up, :, 128:256]),
        )


def three(x):
    hi = x.astype(BF16)
    rest = x - hi.astype(F32)
    mid = rest.astype(BF16)
    low = rest - mid.astype(F32)
    return jnp.concatenate([hi.astype(F32), mid.astype(F32), low, jnp.zeros_like(x)], axis=0).astype(BF16)


def own_forces(near, low, high, pick_ref):
    lane = lanes_of((8, 128))
    sum0 = (near[0] + near[1]) + (near[2] + near[3])
    lo = (low[0] + low[1]) + (low[2] + low[3])
    hi = (high[0] + high[1]) + (high[2] + high[3])
    sum0 = jnp.where(lane < NEAR, sum0, 0.0)
    sum1 = jnp.where(lane < 36, lo, jnp.where(lane < 72, hi, 0.0))
    atom = rows_of((128, 128))
    pick0 = jnp.where(atom == pick_ref[0:1, :], 1.0, 0.0).astype(BF16)
    pick1 = jnp.where(atom == pick_ref[1:2, :], 1.0, 0.0).astype(BF16)
    parts = lax.dot_general(three(sum0), pick0, NT, preferred_element_type=F32)
    parts = parts + lax.dot_general(three(sum1), pick1, NT, preferred_element_type=F32)
    return (parts[0:8] + parts[8:16]) + parts[16:24]


def payload(source, pick_ref):
    return gather(source, pick_ref[0:1, :]), gather(source, pick_ref[1:2, :])


def first_kernel(
    pos_ref, vel_ref, force_ref, spec_ref, live_ref, send_ref, nb_ref, count_ref,
    radial_ref, embed_ref, env_ref, latent_ref, read_ref,
    ext_ref, nball_ref, half_ref, source_ref, pick_ref, w1_ref, lt_ref, li_ref, bw_ref, ew_ref, rad_ref, rc_ref,
    wide, sends, mine, near, low, high, nbs, sems, nbsems,
):
    greet()
    me = lax.axis_index("yz")
    slab, _, _ = partners()
    lane = lanes_of((8, 128))
    row = rows_of((8, 128))

    wide[...] = jnp.zeros_like(wide)
    wide[0, 0:3, 0:ATOMS] = pos_ref[...]
    wide[1, 0:3, 0:ATOMS] = vel_ref[...]
    wide[2, 0:3, 0:ATOMS] = force_ref[...]
    wide[3, 0:1, 0:ATOMS] = spec_ref[...].astype(F32)
    kinds = jnp.broadcast_to(wide[3, 0:1, :], (8, 128))
    half = wide[1] + 0.5 * STEP * inverse_mass(kinds) * wide[2]
    moved = wide[0] + STEP * half
    live = jnp.broadcast_to(live_ref[...].astype(F32), (8, 128))
    source = jnp.where(row < 3, moved, jnp.where(row == 3, kinds, live))
    half_ref[...] = half
    source_ref[...] = source

    sends[...] = jnp.zeros_like(sends)
    sends[:, 0:GHOSTS] = send_ref[...]
    pick0 = jnp.where(lane < ATOMS, lane, 127)
    pick1 = jnp.full((8, 128), 127, I32)
    for block, tile, at in ((3, 0, 48), (4, 0, 60), (0, 1, 0), (1, 1, 12), (2, 1, 24), (5, 1, 36), (6, 1, 48), (7, 1, 60)):
        names = jnp.broadcast_to(sends[block : block + 1, :], (8, 128))
        names = pltpu.roll(names, at, 1) if at else names
        here = (lane >= at) & (lane < at + GHOSTS)
        if tile == 0:
            pick0 = jnp.where(here, names, pick0)
        else:
            pick1 = jnp.where(here, names, pick1)
    pick_ref[...] = jnp.where(row == 0, pick0, pick1)
    tile0, tile1 = payload(source, pick_ref)
    tile0 = jnp.where(row == 4, live, tile0)
    mine[0] = tile0
    mine[1] = tile1
    near[me] = tile0

    diagonal = rows_of((ATOMS, ATOMS)) == lanes_of((ATOMS, ATOMS))
    counts = jnp.sum(jnp.where(diagonal, count_ref[...].astype(F32), 0.0), axis=1, keepdims=True)
    names = nb_ref[...]
    shape = names.shape
    inner = (names >= 84) & (names < 108)
    outer = (names >= ATOMS) & (names < 84)
    names = jnp.where(inner, names - 36, jnp.where(outer, names + 24, names))
    used = (lanes_of(shape).astype(F32) < counts) & (
        rows_of(shape).astype(F32) < jnp.broadcast_to(live_ref[...].astype(F32), shape)
    )
    nbs[me] = jnp.where(used, names, -1)

    greeted()
    copies = spread(lambda q: (mine.at[0], mine.at[1]), near, low, high, sems)
    for s, g, q in slab:
        copies.append(send(nbs.at[me], nbs.at[me], nbsems, s - 1, g, q))

    prepare(radial_ref, embed_ref, env_ref, latent_ref, read_ref, w1_ref, lt_ref, li_ref, bw_ref, ew_ref, rad_ref, rc_ref)

    for copy in copies:
        copy.wait()
    assemble(ext_ref, near, low, high)
    for d in range(N_YZ):
        nball_ref[d * ATOMS : (d + 1) * ATOMS, :] = nbs[d]


def prepare(radial_ref, embed_ref, env_ref, latent_ref, read_ref, w1_ref, lt_ref, li_ref, bw_ref, ew_ref, rad_ref, rc_ref):
    radial = radial_ref[...].astype(F32)
    reads = read_ref[...].astype(F32)
    stack = jnp.concatenate(
        [radial, embed_ref[1].astype(F32), embed_ref[0].astype(F32), jnp.zeros((104, LATENT), F32)], axis=0
    )
    w1_ref[...] = (stack.T * 0.5).astype(BF16)[:, 0:32]
    env = env_ref[0].astype(F32)
    lt_ref[0:FEATURES, :] = env.T.astype(BF16)
    for at in range(0, LATENT, 128):
        rows = latent_ref[0, at : at + 128, :].astype(F32)
        lt_ref[FEATURES : FEATURES + LATENT, at : at + 128] = (rows.T * 0.5).astype(BF16)
        bw_ref[FEATURES + at : FEATURES + at + 128, :] = (rows * (reads * 0.5)).astype(BF16)
    rows = latent_ref[0, LATENT : LATENT + FEATURES, :].astype(F32)
    li_ref[...] = (rows.T * 0.5).astype(BF16)
    bw_ref[0:FEATURES, :] = (rows * (reads * 0.5)).astype(BF16)
    column = jnp.broadcast_to(reads, (128, LATENT)).T
    ew_ref[:, 0:FEATURES] = env_ref[0]
    ew_ref[:, FEATURES : FEATURES + 16] = jnp.where(lanes_of((LATENT, 16)) == 0, column[:, 0:16], 0.0).astype(BF16)
    rad_ref[0:8, :] = (radial * 0.5).astype(BF16)
    rad_ref[8:16, :] = jnp.zeros((8, LATENT), BF16)
    rc_ref[:, 0:128] = column
    rc_ref[:, 128:256] = column


def collect(f_ref, pick_ref, back0, back1, near, low, high, sems):
    me = lax.axis_index("yz")
    greet()
    fold(f_ref, back0, back1)
    near[me] = back0[me]
    greeted()
    for copy in spread(lambda q: (back0.at[q], back1.at[q]), near, low, high, sems):
        copy.wait()
    return own_forces(near, low, high, pick_ref)


def middle_kernel(
    f_ref, half_ref, source_ref, pick_ref,
    ext_ref, half_two_ref, next_ref, end_ref,
    back0, back1, near, low, high, sems, mine, near2, low2, high2, sems2,
):
    me = lax.axis_index("yz")
    row = rows_of((8, 128))
    forces = collect(f_ref, pick_ref, back0, back1, near, low, high, sems)
    source = source_ref[...]
    kick = 0.5 * STEP * inverse_mass(jnp.broadcast_to(source[3:4], (8, 128))) * forces
    half_two = (half_ref[...] + kick) + kick
    source = jnp.where(row < 3, source + STEP * half_two, source)
    tile0, tile1 = payload(source, pick_ref)
    tile0 = jnp.where(row == 4, jnp.broadcast_to(source[4:5], (8, 128)), tile0)
    mine[0] = tile0
    mine[1] = tile1
    near2[me] = tile0
    copies = spread(lambda q: (mine.at[0], mine.at[1]), near2, low2, high2, sems2)
    half_two_ref[...] = half_two
    next_ref[...] = source
    end_ref[...] = source[0:3, 0:ATOMS]
    for copy in copies:
        copy.wait()
    assemble(ext_ref, near2, low2, high2)


def last_kernel(
    f_ref, half_ref, source_ref, pick_ref,
    vel_ref, force_ref,
    back0, back1, near, low, high, sems,
):
    forces = collect(f_ref, pick_ref, back0, back1, near, low, high, sems)
    kick = 0.5 * STEP * inverse_mass(jnp.broadcast_to(source_ref[3:4, :], (8, 128))) * forces
    vel_ref[...] = (half_ref[...] + kick)[0:3, 0:ATOMS]
    force_ref[...] = forces[0:3, 0:ATOMS]


def chain(items, ext_ref, nb_ref, w1_ref, lt_ref, li_ref, bw_ref, ew_ref, rad_ref, rc_ref, f_ref):
    kind = rows_of((8, 128)).astype(F32)
    mid = (kind + 0.5) * 0.125
    geo, inputs = [], []
    for domain, slot, active in items:
        names = nb_ref[pl.ds(domain * ATOMS + slot, 1), :]
        valid = (names >= 0) & active
        names = jnp.maximum(names, 0)
        here = names < NEAR
        place = jnp.where(here, names, names - NEAR)
        tile0 = ext_ref[domain, :, 0:128]
        neigh = jnp.where(here, gather(tile0, place), gather(ext_ref[domain, :, 128:256], place))
        centre = gather(tile0, jnp.full((1, 128), slot, I32))
        u = (neigh - centre) * (1.0 / 6.0)
        sq = u[0:1] * u[0:1] + u[1:2] * u[1:2] + u[2:3] * u[2:3]
        inside = jnp.where(valid, jnp.maximum(1.0 - sq, 0.0), 0.0)
        env = inside * inside
        delta = sq - mid
        basis = jnp.exp(-128.0 * delta * delta)
        theirs = jnp.where(kind == neigh[3:4], 1.0, 0.0)
        own = jnp.where(kind == centre[3:4], 1.0, 0.0)
        inputs.append(jnp.concatenate([basis, theirs, own, jnp.zeros((8, 128), F32)], axis=0).astype(BF16))
        geo.append((names, u, inside, env, basis * delta))
    hp = mm(w1_ref[...], jnp.concatenate(inputs, axis=1)).astype(BF16)
    yield
    y1 = 1.0 + jnp.tanh(hp)
    h0 = hp * y1
    d1 = y1 + h0 * (2.0 - y1)
    yield
    zv = mm(lt_ref[...], h0)
    yield
    inner, kept = [], []
    for c, (names, u, inside, env, slope) in enumerate(geo):
        z = zv[0:FEATURES, c * 128 : c * 128 + 128]
        ue = [u[k : k + 1] * env for k in range(3)]
        c4 = [jnp.sum(z * ue[k], axis=1, keepdims=True) * SCALE for k in range(3)]
        q = c4[0] * ue[0] + c4[1] * ue[1] + c4[2] * ue[2]
        inner.append((z * q).astype(BF16))
        kept.append((z, ue, c4, q))
    yield
    vp = (zv[FEATURES:] + mm(li_ref[...], jnp.concatenate(inner, axis=1))).astype(BF16)
    yield
    y2 = 1.0 + jnp.tanh(vp)
    s2 = vp * y2
    d2 = y2 + s2 * (2.0 - y2)
    p = jnp.sum((h0 + s2).astype(F32) * rc_ref[...], axis=0, keepdims=True)
    yield
    dj = mm(bw_ref[...], d2)
    yield
    sums, dws = [], []
    for c, (names, u, inside, env, slope) in enumerate(geo):
        z, ue, c4, q = kept[c]
        di = dj[0:FEATURES, c * 128 : c * 128 + 128]
        y = di * z
        g = [jnp.sum(y * (ue[k] * env), axis=1, keepdims=True) * SCALE for k in range(3)]
        dws.append(di * q + g[0] * u[0:1] + g[1] * u[1:2] + g[2] * u[2:3])
        ye = y * env
        sums.append([jnp.sum(c4[k] * ye + g[k] * z, axis=0, keepdims=True) for k in range(3)])
    dw = jnp.concatenate(dws, axis=1)
    ones = jnp.ones((8, dw.shape[1]), F32)
    dw = jnp.concatenate([dw, ones, jnp.zeros_like(ones)], axis=0).astype(BF16)
    yield
    a = dj[FEATURES:] + mm(ew_ref[...], dw)
    yield
    db = mm(rad_ref[...], a.astype(BF16) * d1)
    yield
    for c, (names, u, inside, env, slope) in enumerate(geo):
        domain, slot, active = items[c]
        lanes = slice(c * 128, c * 128 + 128)
        s = sums[c]
        dsq = env * jnp.sum(db[0:8, lanes] * slope, axis=0, keepdims=True) * -256.0
        denv = p[:, lanes] + u[0:1] * s[0] + u[1:2] * s[1] + u[2:3] * s[2]
        twice = 2.0 * (dsq - 2.0 * inside * denv)
        rows = [(env * s[k] + u[k : k + 1] * twice) * (1.0 / 6.0) for k in range(3)]
        du = jnp.concatenate(rows + [jnp.zeros((5, 128), F32)], axis=0)
        hi = du.astype(BF16)
        parts = jnp.concatenate([hi.astype(F32), du - hi.astype(F32)], axis=0).astype(BF16)
        pick = jnp.where(rows_of((EXT, 128)) == names, 1.0, 0.0).astype(BF16)
        out = lax.dot_general(parts, pick, NT, preferred_element_type=F32)
        out = out[0:8] + out[8:16]
        total = jnp.sum(du, axis=1, keepdims=True)
        f_ref[domain] += jnp.where(lanes_of((8, EXT)) == slot, total, 0.0) - out
    yield


def pair_kernel(ext_ref, nb_ref, w1_ref, lt_ref, li_ref, bw_ref, ew_ref, rad_ref, rc_ref, f_ref, sums):
    sums[...] = jnp.zeros_like(sums)
    ends = []
    total = jnp.int32(0)
    for d in range(N_YZ):
        total = total + jnp.max(ext_ref[d, 4:5, 0:1]).astype(I32)
        ends.append(total)
    me = lax.axis_index("yz")
    first = (total * me) // N_YZ
    last = (total * (me + 1)) // N_YZ
    steps = (last - first + 2 * CHAINS - 1) // (2 * CHAINS)

    def step(b, carry):
        chains = []
        for g in range(CHAINS):
            items = []
            for c in range(2):
                at = first + (b * CHAINS + g) * 2 + c
                active = at < last
                at = jnp.minimum(at, total - 1)
                domain = sum((at >= e).astype(I32) for e in ends[:-1])
                base = jnp.where(at >= ends[2], ends[2], jnp.where(at >= ends[1], ends[1], jnp.where(at >= ends[0], ends[0], 0)))
                items.append((domain, at - base, active))
            chains.append(chain(items, ext_ref, nb_ref, w1_ref, lt_ref, li_ref, bw_ref, ew_ref, rad_ref, rc_ref, sums))
        while chains:
            chains = [one for one in chains if next(one, chains) is not chains]
        return carry

    lax.fori_loop(0, steps, step, 0)
    lane = lanes_of((8, 128))
    for d in range(N_YZ):
        tile0 = sums[d, :, 0:128]
        f_ref[d, :, 0:128] = jnp.where(lane < NEAR, tile0, 0.0)
        tail = jnp.concatenate([sums[d, :, 128:EXT], jnp.zeros((8, 256 - EXT), F32)], axis=1)
        far = jnp.where(lane < 128 - NEAR, pltpu.roll(tile0, 128 - NEAR, 1), pltpu.roll(tail, 128 - NEAR, 1))
        f_ref[d, :, 128:256] = jnp.where(lane < NEAR, far, 0.0)


def body(
    positions, velocities, forces_start, species, live_atoms, send_list, neighbours, neighbour_count,
    radial_weight, species_embed, env_weight, latent_weight, readout,
):
    vm = pl.BlockSpec(memory_space=pltpu.VMEM)
    tile = jax.ShapeDtypeStruct((8, 128), F32)
    lists = jax.ShapeDtypeStruct((N_YZ, 8, 256), F32)
    atoms = jax.ShapeDtypeStruct((3, ATOMS), F32)
    four = pltpu.VMEM((N_YZ, 8, 128), F32)
    copies = pltpu.SemaphoreType.DMA((2, 3 * N_YZ - 1))
    params = functools.partial(pltpu.CompilerParams, vmem_limit_bytes=48 << 20)

    args = (
        positions, velocities, forces_start, species.reshape(1, -1), live_atoms.reshape(1, 1), send_list, neighbours,
        neighbour_count.reshape(1, -1), radial_weight, species_embed, env_weight, latent_weight, readout.reshape(1, -1),
    )
    weights = [(LATENT, 32), (FEATURES + LATENT, LATENT), (LATENT, FEATURES), (FEATURES + LATENT, LATENT), (LATENT, FEATURES + 16), (16, LATENT)]
    out_shape = [lists, jax.ShapeDtypeStruct((N_YZ * ATOMS, SLOTS), I32), tile, tile, jax.ShapeDtypeStruct((8, 128), I32)]
    out_shape += [jax.ShapeDtypeStruct(s, BF16) for s in weights] + [jax.ShapeDtypeStruct((LATENT, 256), F32)]
    ext, names, half, source, pick, *prepared = pl.pallas_call(
        first_kernel,
        out_shape=out_shape,
        in_specs=[vm] * len(args),
        out_specs=[vm] * len(out_shape),
        scratch_shapes=[
            pltpu.VMEM((4, 8, 128), F32), pltpu.VMEM((8, 128), I32), pltpu.VMEM((2, 8, 128), F32), four, four, four,
            pltpu.VMEM((N_YZ, ATOMS, SLOTS), I32), copies, pltpu.SemaphoreType.DMA((2, N_YZ - 1)),
        ],
        compiler_params=params(collective_id=0, has_side_effects=True),
    )(*args)

    def forces_of(ext):
        return pl.pallas_call(
            pair_kernel,
            out_shape=lists,
            in_specs=[vm] * 9,
            out_specs=vm,
            scratch_shapes=[pltpu.VMEM((N_YZ, 8, EXT), F32)],
            compiler_params=params(),
        )(ext, names, *prepared)

    returning = [four] * 5 + [copies]
    ext, half, source, positions_end = pl.pallas_call(
        middle_kernel,
        out_shape=[lists, tile, tile, atoms],
        in_specs=[vm] * 4,
        out_specs=[vm] * 4,
        scratch_shapes=returning + [pltpu.VMEM((2, 8, 128), F32), four, four, four, copies],
        compiler_params=params(collective_id=1, has_side_effects=True),
    )(forces_of(ext), half, source, pick)

    velocities_end, forces_end = pl.pallas_call(
        last_kernel,
        out_shape=[atoms, atoms],
        in_specs=[vm] * 4,
        out_specs=[vm] * 2,
        scratch_shapes=returning,
        compiler_params=params(collective_id=2, has_side_effects=True),
    )(forces_of(ext), half, source, pick)
    return positions_end, velocities_end, forces_end


def solution(mesh):
    both = ("gx", "yz")
    atom = P(None, both)
    return jax.shard_map(
        body,
        mesh=mesh,
        in_specs=(atom, atom, atom, P(both), P(both), atom, P(both, None), P(both), P(), P(), P(), P(), P()),
        out_specs=(atom, atom, atom),
        check_vma=False,
    )
```

time: 401 us -> 64.8 us (0.16); the launches traced: 394 us -> 64.6 us
  matrix products: 162 us -> 0 us
  local copies, waits for them, and re-layouts: 108 us -> 4.53 us
  other arithmetic: 67.9 us -> 0 us
  Pallas kernels: 0 us -> 58.6 us
  starting transfers between devices: 40.5 us -> 0 us
  waiting for transfers between devices: 10.1 us -> 0 us
    dot_general x244 -> x0, matrix products: 162 us -> none  [the longest x24 40.2 us: block_energy(): jnp.dot(neigh_kind, species_embed[1], preferred_element_type=jnp.float32)]
    pallas_call x0 -> x5, Pallas kernels: none -> 58.6 us  [the longest x1 17.8 us: body(): pl.pallas_call(middle_kernel, out_shape=[lists, tile, tile, atoms], in_sp...]
    while x312 -> x0, local copies, waits for them, and re-layouts: 43.4 us -> none
    ppermute x16 -> x0, starting transfers between devices: 40.5 us -> none  [the longest x8 32.8 us: padded(): lax.ppermute(head, axis, [((i + 1) % count, i) for i in range(count)])]
    reduce_sum x144 -> x0, other arithmetic: 23.1 us -> none  [the longest x24 6.99 us: block_energy(): tensor = vectors[:, :, None] * weights[None, :, :]]
    dynamic_slice x48 -> x0, local copies, waits for them, and re-layouts: 19.4 us -> none  [the longest x24 17.6 us: block_update(): block_counts = lax.dynamic_slice_in_dim(counts, first, CENTRES, 0)]
    eq x25 -> x0, local copies, waits for them, and re-layouts: 17.3 us -> none  [the longest x24 16.6 us: block_update(): neigh_idx.reshape(-1)[:, None]]
    lt x24 -> x0, other arithmetic: 17 us -> none  [block_update(): alive_rows = first + jnp.arange(CENTRES, dtype=jnp.int32) < live_count]
  transfers between devices with their start and end apart: 16 -> 0, of which waited for: 10 -> 0; matrix products, arithmetic and copies ran while one was open for 1% -> 0% of each run, Pallas kernels for 0% -> 0%
where the time goes in v1:
time: 64.8 us; the launch traced here: 64.6 us
  Pallas kernels  58.6 us (90%)
  local copies, waits for them, and re-layouts  4.53 us (7%)
  between operations  1.45 us (2%)
    pallas_call x1, Pallas kernels, body(): pl.pallas_call(middle_kernel, out_shape=[lists, tile, tile, atoms], in_sp...  17.8 us
    pallas_call x2, Pallas kernels, forces_of(): pl.pallas_call(pair_kernel, out_shape=lists, in_specs=[vm] * 9, out_specs...  17.6 us
    pallas_call x1, Pallas kernels, body(): pl.pallas_call(first_kernel, out_shape=out_shape, in_specs=[vm] * len(arg...  13.3 us
    pallas_call x1, Pallas kernels, body(): pl.pallas_call(last_kernel, out_shape=[atoms, atoms], in_specs=[vm] * 4,...  9.82 us
    unnamed x26, local copies, waits for them, and re-layouts  4.53 us

profile of v1, /device:TPU:1, one launch (start us, length us, event | category | flops | bytes accessed | tf_op | source)
XLA Modules:
  0.0 64.6 jit_solution(2814310088951644073)
XLA Ops:
  1.3 0.0 copy-start.10
  1.3 0.7 %copy-done.10 = bf16[512]{0:T(512)(128)(2,1)S(1)} copy-done((bf16[512]{0:T(512)(128)(2,1)S(1)}, bf16[512]{0:T(512)(128)(2,1)}, u32[]{:S(2)}) %copy-start.10) | copy-done | bytes 1048
  2.0 0.0 copy-start.1
  2.0 0.0 copy-start.2
  2.0 0.0 copy-start.3
  2.0 0.0 copy-start.4
  2.0 0.0 copy-start.5
  2.0 0.0 copy-start.6
  2.0 0.0 copy-start.7
  2.0 0.0 copy-start.8
  2.0 0.0 copy-start.9
  2.0 1.0 %copy.16.env_ref = bf16[1,512,64]{2,1,0:T(8,128)(2,1)S(1)} copy(bf16[1,512,64]{1,2,0:T(8,128)(2,1)} %param.23) | data formatting | bytes 131072 | tf_op args[10]
  3.1 0.0 copy-done.1
  3.1 0.0 copy-done.2
  3.1 0.0 copy-done.3
  3.1 0.0 copy-done.4
  3.1 0.0 copy-done.5
  3.1 0.0 copy-done.6
  3.1 0.0 copy-done.7
  3.1 0.0 copy-done.8
  3.1 0.0 copy-done.9
  3.2 0.0 copy-start
  3.2 1.1 %copy-done = bf16[1,576,512]{2,1,0:T(8,128)(2,1)S(1)} copy-done((bf16[1,576,512]{2,1,0:T(8,128)(2,1)S(1)}, bf16[1,576,512]{2,1,0:T(8,128)(2,1)}, u32[]{:S(2)}) %copy-start) | copy-done | bytes 589848
  4.2 13.3 %shard_map.148 = (f32[4,8,256]{2,1,0:T(8,128)S(1)}, s32[192,128]{1,0:T(8,128)S(1)}, f32[8,128]{1,0:T(8,128)S(1)}, f32[8,128]{1,0:T(8,128)S(1)}, s32[8,128]{1,0:T...) custom-call(f32[3,48]{1,0:T(4,128)S(1)} %copy-done.5, ...), custom_call_target="tpu_custom_call" | custom-call | tf_op jit(solution)/shard_map/pallas_call | solution.py:439
  17.5 8.8 %shard_map.149.f_ref = f32[4,8,256]{2,1,0:T(8,128)S(1)} custom-call(f32[4,8,256]{2,1,0:T(8,128)S(1)} %get-tuple-element.21.ext_ref, s32[192,128]{1,0:T(8,128)S(1)} %get-tuple-element.22.nb_ref, bf16[512,32]{1,0:T(8,128)(2,1)S(1)} %get-tuple-element.23.w1_ref, bf16[576,512]{1,0:T(8,128)(2,1)S(1)} %get-tuple-element.24.lt_ref, ...), custom_call_target="tpu_custom_call" | custom-call | tf_op jit(solution)/shard_map/pallas_call | solution.py:452
  26.4 17.8 %shard_map.150 = (f32[4,8,256]{2,1,0:T(8,128)S(1)}, f32[8,128]{1,0:T(8,128)S(1)}, f32[8,128]{1,0:T(8,128)S(1)}, f32[3,48]{1,0:T(4,128)S(1)}) custom-call(f32[4,8,256]{2,1,0:T(8,128)S(1)} %shard_map.149.f_ref, f32[8,128]{1,0:T(8,128)S(1)} %get-tuple-element.30.half_ref, f32[8,128]{1,0:T(8,128)S(1)} %get-tuple-element.31.source_ref, ...), custom_call_target="tpu_custom_call" | custom-call | tf_op jit(solution)/shard_map/pallas_call | solution.py:462
  44.2 8.8 %shard_map.151.f_ref = f32[4,8,256]{2,1,0:T(8,128)S(1)} custom-call(f32[4,8,256]{2,1,0:T(8,128)S(1)} %get-tuple-element.34.ext_ref, s32[192,128]{1,0:T(8,128)S(1)} %get-tuple-element.22.nb_ref, bf16[512,32]{1,0:T(8,128)(2,1)S(1)} %get-tuple-element.23.w1_ref, bf16[576,512]{1,0:T(8,128)(2,1)S(1)} %get-tuple-element.24.lt_ref, ...), custom_call_target="tpu_custom_call" | custom-call | tf_op jit(solution)/shard_map/pallas_call | solution.py:452
  53.0 9.8 %shard_map.152 = (f32[3,48]{1,0:T(4,128)S(1)}, f32[3,48]{1,0:T(4,128)S(1)}) custom-call(f32[4,8,256]{2,1,0:T(8,128)S(1)} %shard_map.151.f_ref, f32[8,128]{1,0:T(8,128)S(1)} %get-tuple-element.35.half_ref, f32[8,128]{1,0:T(8,128)S(1)} %get-tuple-element.36.source_ref, s32[8,128]{1,0:T(8,128)S(1)} %get-tuple-element.32.pick_ref), custom_call_target="tpu_custom_call" | custom-call | tf_op jit(solution)/shard_map/pallas_call | solution.py:471
  62.9 0.6 copy.21
  63.4 0.6 copy.22
  64.0 0.6 copy.23
  (1 shorter events, 0.0 us)
Async XLA Ops:
  1.3 0.7 %copy-start.10 = (bf16[512]{0:T(512)(128)(2,1)S(1)}, bf16[512]{0:T(512)(128)(2,1)}, u32[]{:S(2)}) copy-start(bf16[512]{0:T(512)(128)(2,1)} %param.25) | copy-start | bytes 3076
  2.0 1.1 %copy-start.1 = (s32[48,128]{1,0:T(8,128)S(1)}, s32[48,128]{1,0:T(8,128)}, u32[]{:S(2)}) copy-start(s32[48,128]{1,0:T(8,128)} %nb_ref.1) | copy-start | bytes 73732
  2.0 1.1 %copy-start.2 = (bf16[2,8,512]{2,1,0:T(8,128)(2,1)S(1)}, bf16[2,8,512]{2,1,0:T(8,128)(2,1)}, u32[]{:S(2)}) copy-start(bf16[2,8,512]{2,1,0:T(8,128)(2,1)} %embed_ref.1) | copy-start | bytes 49156
  2.0 1.1 %copy-start.3 = (bf16[8,512]{1,0:T(8,128)(2,1)S(1)}, bf16[8,512]{1,0:T(8,128)(2,1)}, u32[]{:S(2)}) copy-start(bf16[8,512]{1,0:T(8,128)(2,1)} %radial_ref.1) | copy-start | bytes 24580
  2.0 1.1 %copy-start.4 = (s32[8,12]{1,0:T(8,128)S(1)}, s32[8,12]{1,0:T(8,128)}, u32[]{:S(2)}) copy-start(s32[8,12]{1,0:T(8,128)} %send_ref.1) | copy-start | bytes 1156
  2.0 1.1 %copy-start.5 = (f32[3,48]{1,0:T(4,128)S(1)}, f32[3,48]{1,0:T(4,128)}, u32[]{:S(2)}) copy-start(f32[3,48]{1,0:T(4,128)} %pos_ref.1) | copy-start | bytes 1732
  2.0 1.1 %copy-start.6 = (f32[3,48]{1,0:T(4,128)S(1)}, f32[3,48]{1,0:T(4,128)}, u32[]{:S(2)}) copy-start(f32[3,48]{1,0:T(4,128)} %vel_ref.1) | copy-start | bytes 1732
  2.0 1.1 %copy-start.7 = (f32[3,48]{1,0:T(4,128)S(1)}, f32[3,48]{1,0:T(4,128)}, u32[]{:S(2)}) copy-start(f32[3,48]{1,0:T(4,128)} %force_ref.1) | copy-start | bytes 1732
  2.0 1.1 %copy-start.8 = (s32[48]{0:T(128)S(1)}, s32[48]{0:T(128)}, u32[]{:S(2)}) copy-start(s32[48]{0:T(128)} %param.16) | copy-start | bytes 580
  2.0 1.1 %copy-start.9 = (s32[48]{0:T(128)S(1)}, s32[48]{0:T(128)}, u32[]{:S(2)}) copy-start(s32[48]{0:T(128)} %param.20) | copy-start | bytes 580
  3.2 1.1 %copy-start = (bf16[1,576,512]{2,1,0:T(8,128)(2,1)S(1)}, bf16[1,576,512]{2,1,0:T(8,128)(2,1)}, u32[]{:S(2)}) copy-start(bf16[1,576,512]{2,1,0:T(8,128)(2,1)} %latent_ref.1) | copy-start | bytes 1769476

commit v2 on v1

--- a/solution.py
+++ b/solution.py
@@ -22,7 +22,8 @@
 LATENT = 512
 FEATURES = 64
 SCALE = 4.0 / SLOTS**0.5
-CHAINS = 4
+CHAINS = 6
+SURE = 12
 
 
 def mm(a, b):
@@ -132,13 +133,16 @@
     return jnp.concatenate([hi.astype(F32), mid.astype(F32), low, jnp.zeros_like(x)], axis=0).astype(BF16)
 
 
-def own_forces(near, low, high, pick_ref):
+def gathered(near, low, high):
     lane = lanes_of((8, 128))
     sum0 = (near[0] + near[1]) + (near[2] + near[3])
     lo = (low[0] + low[1]) + (low[2] + low[3])
     hi = (high[0] + high[1]) + (high[2] + high[3])
     sum0 = jnp.where(lane < NEAR, sum0, 0.0)
-    sum1 = jnp.where(lane < 36, lo, jnp.where(lane < 72, hi, 0.0))
+    return sum0, jnp.where(lane < 36, lo, jnp.where(lane < 72, hi, 0.0))
+
+
+def own_forces(sum0, sum1, pick_ref):
     atom = rows_of((128, 128))
     pick0 = jnp.where(atom == pick_ref[0:1, :], 1.0, 0.0).astype(BF16)
     pick1 = jnp.where(atom == pick_ref[1:2, :], 1.0, 0.0).astype(BF16)
@@ -152,12 +156,15 @@
 
 
 def first_kernel(
-    pos_ref, vel_ref, force_ref, spec_ref, live_ref, send_ref, nb_ref, count_ref,
-    radial_ref, embed_ref, env_ref, latent_ref, read_ref,
+    in_refs,
     ext_ref, nball_ref, half_ref, source_ref, pick_ref, w1_ref, lt_ref, li_ref, bw_ref, ew_ref, rad_ref, rc_ref,
-    wide, sends, mine, near, low, high, nbs, sems, nbsems,
+    wide, sends, mine, near, low, high, nbs, sems, nbsems, latent, landed,
 ):
     greet()
+    pos_ref, vel_ref, force_ref, spec_ref, live_ref, send_ref, nb_ref, count_ref = in_refs[:8]
+    radial_ref, embed_ref, env_ref, latent_ref, read_ref = in_refs[8:]
+    load = pltpu.make_async_copy(latent_ref, latent, landed)
+    load.start()
     me = lax.axis_index("yz")
     slab, _, _ = partners()
     lane = lanes_of((8, 128))
@@ -212,7 +219,8 @@
     for s, g, q in slab:
         copies.append(send(nbs.at[me], nbs.at[me], nbsems, s - 1, g, q))
 
-    prepare(radial_ref, embed_ref, env_ref, latent_ref, read_ref, w1_ref, lt_ref, li_ref, bw_ref, ew_ref, rad_ref, rc_ref)
+    load.wait()
+    prepare(radial_ref, embed_ref, env_ref, latent, read_ref, w1_ref, lt_ref, li_ref, bw_ref, ew_ref, rad_ref, rc_ref)
 
     for copy in copies:
         copy.wait()
@@ -223,13 +231,12 @@
 
 def prepare(radial_ref, embed_ref, env_ref, latent_ref, read_ref, w1_ref, lt_ref, li_ref, bw_ref, ew_ref, rad_ref, rc_ref):
     radial = radial_ref[...].astype(F32)
-    reads = read_ref[...].astype(F32)
+    reads = read_ref[...].astype(F32).reshape(1, LATENT)
     stack = jnp.concatenate(
         [radial, embed_ref[1].astype(F32), embed_ref[0].astype(F32), jnp.zeros((104, LATENT), F32)], axis=0
     )
     w1_ref[...] = (stack.T * 0.5).astype(BF16)[:, 0:32]
-    env = env_ref[0].astype(F32)
-    lt_ref[0:FEATURES, :] = env.T.astype(BF16)
+    lt_ref[0:FEATURES, :] = env_ref[0].astype(F32).T.astype(BF16)
     for at in range(0, LATENT, 128):
         rows = latent_ref[0, at : at + 128, :].astype(F32)
         lt_ref[FEATURES : FEATURES + LATENT, at : at + 128] = (rows.T * 0.5).astype(BF16)
@@ -242,29 +249,29 @@
     ew_ref[:, FEATURES : FEATURES + 16] = jnp.where(lanes_of((LATENT, 16)) == 0, column[:, 0:16], 0.0).astype(BF16)
     rad_ref[0:8, :] = (radial * 0.5).astype(BF16)
     rad_ref[8:16, :] = jnp.zeros((8, LATENT), BF16)
-    rc_ref[:, 0:128] = column
-    rc_ref[:, 128:256] = column
-
-
-def collect(f_ref, pick_ref, back0, back1, near, low, high, sems):
+    rc_ref[...] = column
+
+
+def collect(f_ref, refs, fsum, own, back0, back1, near, low, high, sems):
     me = lax.axis_index("yz")
     greet()
-    fold(f_ref, back0, back1)
+    sure_forces(fsum, own, f_ref, refs)
+    fold(fsum, back0, back1)
     near[me] = back0[me]
     greeted()
     for copy in spread(lambda q: (back0.at[q], back1.at[q]), near, low, high, sems):
         copy.wait()
-    return own_forces(near, low, high, pick_ref)
+    return gathered(near, low, high)
 
 
 def middle_kernel(
-    f_ref, half_ref, source_ref, pick_ref,
-    ext_ref, half_two_ref, next_ref, end_ref,
-    back0, back1, near, low, high, sems, mine, near2, low2, high2, sems2,
+    f_ref, half_ref, source_ref, pick_ref, *rest
 ):
+    refs, (next_ext_ref, half_two_ref, next_ref), scratch = rest[:9], rest[9:12], rest[12:]
+    mine, near, low, high, sems = scratch[8:]
     me = lax.axis_index("yz")
     row = rows_of((8, 128))
-    forces = collect(f_ref, pick_ref, back0, back1, near, low, high, sems)
+    forces = own_forces(*collect(f_ref, refs, *scratch[:8]), pick_ref)
     source = source_ref[...]
     kick = 0.5 * STEP * inverse_mass(jnp.broadcast_to(source[3:4], (8, 128))) * forces
     half_two = (half_ref[...] + kick) + kick
@@ -273,28 +280,29 @@
     tile0 = jnp.where(row == 4, jnp.broadcast_to(source[4:5], (8, 128)), tile0)
     mine[0] = tile0
     mine[1] = tile1
-    near2[me] = tile0
-    copies = spread(lambda q: (mine.at[0], mine.at[1]), near2, low2, high2, sems2)
+    near[me] = tile0
+    copies = spread(lambda q: (mine.at[0], mine.at[1]), near, low, high, sems)
     half_two_ref[...] = half_two
     next_ref[...] = source
-    end_ref[...] = source[0:3, 0:ATOMS]
     for copy in copies:
         copy.wait()
-    assemble(ext_ref, near2, low2, high2)
-
-
-def last_kernel(
-    f_ref, half_ref, source_ref, pick_ref,
-    vel_ref, force_ref,
-    back0, back1, near, low, high, sems,
-):
-    forces = collect(f_ref, pick_ref, back0, back1, near, low, high, sems)
+    assemble(next_ext_ref, near, low, high)
+
+
+def last_kernel(f_ref, *rest):
+    refs, total_ref, scratch = rest[:9], rest[9], rest[10:]
+    total_ref[0], total_ref[1] = collect(f_ref, refs, *scratch)
+
+
+def end_kernel(total_ref, half_ref, source_ref, pick_ref, pos_ref, vel_ref, force_ref):
+    forces = own_forces(total_ref[0], total_ref[1], pick_ref)
     kick = 0.5 * STEP * inverse_mass(jnp.broadcast_to(source_ref[3:4, :], (8, 128))) * forces
+    pos_ref[...] = source_ref[0:3, 0:ATOMS]
     vel_ref[...] = (half_ref[...] + kick)[0:3, 0:ATOMS]
     force_ref[...] = forces[0:3, 0:ATOMS]
 
 
-def chain(items, ext_ref, nb_ref, w1_ref, lt_ref, li_ref, bw_ref, ew_ref, rad_ref, rc_ref, f_ref):
+def chain(items, add, ext_ref, nb_ref, w1_ref, lt_ref, li_ref, bw_ref, ew_ref, rad_ref, rc_ref):
     kind = rows_of((8, 128)).astype(F32)
     mid = (kind + 0.5) * 0.125
     geo, inputs = [], []
@@ -339,7 +347,8 @@
     y2 = 1.0 + jnp.tanh(vp)
     s2 = vp * y2
     d2 = y2 + s2 * (2.0 - y2)
-    p = jnp.sum((h0 + s2).astype(F32) * rc_ref[...], axis=0, keepdims=True)
+    h2 = (h0 + s2).astype(F32)
+    p = [jnp.sum(h2[:, c * 128 : c * 128 + 128] * rc_ref[...], axis=0, keepdims=True) for c in range(len(geo))]
     yield
     dj = mm(bw_ref[...], d2)
     yield
@@ -365,7 +374,7 @@
         lanes = slice(c * 128, c * 128 + 128)
         s = sums[c]
         dsq = env * jnp.sum(db[0:8, lanes] * slope, axis=0, keepdims=True) * -256.0
-        denv = p[:, lanes] + u[0:1] * s[0] + u[1:2] * s[1] + u[2:3] * s[2]
+        denv = p[c] + u[0:1] * s[0] + u[1:2] * s[1] + u[2:3] * s[2]
         twice = 2.0 * (dsq - 2.0 * inside * denv)
         rows = [(env * s[k] + u[k : k + 1] * twice) * (1.0 / 6.0) for k in range(3)]
         du = jnp.concatenate(rows + [jnp.zeros((5, 128), F32)], axis=0)
@@ -375,46 +384,82 @@
         out = lax.dot_general(parts, pick, NT, preferred_element_type=F32)
         out = out[0:8] + out[8:16]
         total = jnp.sum(du, axis=1, keepdims=True)
-        f_ref[domain] += jnp.where(lanes_of((8, EXT)) == slot, total, 0.0) - out
-    yield
+        add(domain, jnp.where(lanes_of((8, EXT)) == slot, total, 0.0) - out)
+    yield
+
+
+def drive(chains):
+    while chains:
+        chains = [one for one in chains if next(one, chains) is not chains]
+
+
+def split(tile0, tail):
+    lane = lanes_of((8, 128))
+    far = jnp.where(lane < 128 - NEAR, pltpu.roll(tile0, 128 - NEAR, 1), pltpu.roll(tail, 128 - NEAR, 1))
+    return jnp.where(lane < NEAR, tile0, 0.0), jnp.where(lane < NEAR, far, 0.0)
 
 
 def pair_kernel(ext_ref, nb_ref, w1_ref, lt_ref, li_ref, bw_ref, ew_ref, rad_ref, rc_ref, f_ref, sums):
+    refs = (ext_ref, nb_ref, w1_ref, lt_ref, li_ref, bw_ref, ew_ref, rad_ref, rc_ref)
     sums[...] = jnp.zeros_like(sums)
     ends = []
     total = jnp.int32(0)
     for d in range(N_YZ):
-        total = total + jnp.max(ext_ref[d, 4:5, 0:1]).astype(I32)
+        total = total + jnp.max(ext_ref[d, 4:5, 0:1]).astype(I32) - SURE
         ends.append(total)
     me = lax.axis_index("yz")
     first = (total * me) // N_YZ
     last = (total * (me + 1)) // N_YZ
-    steps = (last - first + 2 * CHAINS - 1) // (2 * CHAINS)
-
-    def step(b, carry):
-        chains = []
-        for g in range(CHAINS):
+    steps = lax.max(last - first + CHAINS - 1, 0) // (2 * CHAINS)
+
+    def add(domain, value):
+        sums[domain, :, 0:EXT] += value
+
+    def work(start, chains):
+        made = []
+        for g in range(chains):
             items = []
             for c in range(2):
-                at = first + (b * CHAINS + g) * 2 + c
+                at = start + 2 * g + c
                 active = at < last
                 at = jnp.minimum(at, total - 1)
                 domain = sum((at >= e).astype(I32) for e in ends[:-1])
-                base = jnp.where(at >= ends[2], ends[2], jnp.where(at >= ends[1], ends[1], jnp.where(at >= ends[0], ends[0], 0)))
-                items.append((domain, at - base, active))
-            chains.append(chain(items, ext_ref, nb_ref, w1_ref, lt_ref, li_ref, bw_ref, ew_ref, rad_ref, rc_ref, sums))
-        while chains:
-            chains = [one for one in chains if next(one, chains) is not chains]
+                base = jnp.where(at >= ends[0], ends[0], 0)
+                for e in ends[1:-1]:
+                    base = jnp.where(at >= e, e, base)
+                items.append((domain, at - base + SURE, active))
+            made.append(chain(items, add, *refs))
+        drive(made)
+
+    def step(b, carry):
+        work(first + b * 2 * CHAINS, CHAINS)
         return carry
 
     lax.fori_loop(0, steps, step, 0)
-    lane = lanes_of((8, 128))
+    rest = first + steps * 2 * CHAINS
+
+    @pl.when(rest < last)
+    def _():
+        work(rest, CHAINS // 2)
+
     for d in range(N_YZ):
-        tile0 = sums[d, :, 0:128]
-        f_ref[d, :, 0:128] = jnp.where(lane < NEAR, tile0, 0.0)
-        tail = jnp.concatenate([sums[d, :, 128:EXT], jnp.zeros((8, 256 - EXT), F32)], axis=1)
-        far = jnp.where(lane < 128 - NEAR, pltpu.roll(tile0, 128 - NEAR, 1), pltpu.roll(tail, 128 - NEAR, 1))
-        f_ref[d, :, 128:256] = jnp.where(lane < NEAR, far, 0.0)
+        f_ref[d, :, 0:128], f_ref[d, :, 128:256] = split(sums[d, :, 0:128], sums[d, :, 128:256])
+
+
+def sure_forces(fsum, own, f_ref, refs):
+    me = lax.axis_index("yz")
+    values = []
+    chains = []
+    for g in range(SURE // 2):
+        items = [(me, 2 * g + c, True) for c in range(2)]
+        chains.append(chain(items, lambda domain, value: values.append(value), *refs))
+    drive(chains)
+    own[...] = jnp.zeros_like(own)
+    own[:, 0:EXT] = functools.reduce(jnp.add, values)
+    fsum[...] = f_ref[...]
+    tile0, tile1 = split(own[:, 0:128], own[:, 128:256])
+    fsum[me, :, 0:128] += tile0
+    fsum[me, :, 128:256] += tile1
 
 
 def body(
@@ -426,26 +471,34 @@
     lists = jax.ShapeDtypeStruct((N_YZ, 8, 256), F32)
     atoms = jax.ShapeDtypeStruct((3, ATOMS), F32)
     four = pltpu.VMEM((N_YZ, 8, 128), F32)
+    sums = pltpu.VMEM((N_YZ, 8, 256), F32)
     copies = pltpu.SemaphoreType.DMA((2, 3 * N_YZ - 1))
     params = functools.partial(pltpu.CompilerParams, vmem_limit_bytes=48 << 20)
 
     args = (
         positions, velocities, forces_start, species.reshape(1, -1), live_atoms.reshape(1, 1), send_list, neighbours,
-        neighbour_count.reshape(1, -1), radial_weight, species_embed, env_weight, latent_weight, readout.reshape(1, -1),
+        neighbour_count.reshape(1, -1), radial_weight, species_embed, env_weight, latent_weight,
+        readout,
     )
     weights = [(LATENT, 32), (FEATURES + LATENT, LATENT), (LATENT, FEATURES), (FEATURES + LATENT, LATENT), (LATENT, FEATURES + 16), (16, LATENT)]
     out_shape = [lists, jax.ShapeDtypeStruct((N_YZ * ATOMS, SLOTS), I32), tile, tile, jax.ShapeDtypeStruct((8, 128), I32)]
-    out_shape += [jax.ShapeDtypeStruct(s, BF16) for s in weights] + [jax.ShapeDtypeStruct((LATENT, 256), F32)]
+    out_shape += [jax.ShapeDtypeStruct(s, BF16) for s in weights] + [jax.ShapeDtypeStruct((LATENT, 128), F32)]
+    scratch = [
+        pltpu.VMEM((4, 8, 128), F32), pltpu.VMEM((8, 128), I32), pltpu.VMEM((2, 8, 128), F32), four, four, four,
+        pltpu.VMEM((N_YZ, ATOMS, SLOTS), I32), copies, pltpu.SemaphoreType.DMA((2, N_YZ - 1)),
+        pltpu.VMEM(latent_weight.shape, BF16), pltpu.SemaphoreType.DMA,
+    ]
+
+    def first(*refs):
+        first_kernel(refs[: len(args)], *refs[len(args) :])
+
     ext, names, half, source, pick, *prepared = pl.pallas_call(
-        first_kernel,
+        first,
         out_shape=out_shape,
-        in_specs=[vm] * len(args),
+        in_specs=[vm] * 11 + [pl.BlockSpec(memory_space=pl.ANY), vm],
         out_specs=[vm] * len(out_shape),
-        scratch_shapes=[
-            pltpu.VMEM((4, 8, 128), F32), pltpu.VMEM((8, 128), I32), pltpu.VMEM((2, 8, 128), F32), four, four, four,
-            pltpu.VMEM((N_YZ, ATOMS, SLOTS), I32), copies, pltpu.SemaphoreType.DMA((2, N_YZ - 1)),
-        ],
-        compiler_params=params(collective_id=0, has_side_effects=True),
+        scratch_shapes=scratch,
+        compiler_params=pltpu.CompilerParams(vmem_limit_bytes=103 << 19, collective_id=0, has_side_effects=True),
     )(*args)
 
     def forces_of(ext):
@@ -454,29 +507,36 @@
             out_shape=lists,
             in_specs=[vm] * 9,
             out_specs=vm,
-            scratch_shapes=[pltpu.VMEM((N_YZ, 8, EXT), F32)],
+            scratch_shapes=[sums],
             compiler_params=params(),
         )(ext, names, *prepared)
 
-    returning = [four] * 5 + [copies]
-    ext, half, source, positions_end = pl.pallas_call(
+    returning = [sums, pltpu.VMEM((8, 256), F32)] + [four] * 5 + [copies]
+    next_ext, half, source = pl.pallas_call(
         middle_kernel,
-        out_shape=[lists, tile, tile, atoms],
-        in_specs=[vm] * 4,
-        out_specs=[vm] * 4,
+        out_shape=[lists, tile, tile],
+        in_specs=[vm] * 13,
+        out_specs=[vm] * 3,
         scratch_shapes=returning + [pltpu.VMEM((2, 8, 128), F32), four, four, four, copies],
         compiler_params=params(collective_id=1, has_side_effects=True),
-    )(forces_of(ext), half, source, pick)
-
-    velocities_end, forces_end = pl.pallas_call(
+    )(forces_of(ext), half, source, pick, ext, names, *prepared)
+
+    totals = pl.pallas_call(
         last_kernel,
-        out_shape=[atoms, atoms],
-        in_specs=[vm] * 4,
-        out_specs=[vm] * 2,
+        out_shape=jax.ShapeDtypeStruct((2, 8, 128), F32),
+        in_specs=[vm] * 10,
+        out_specs=vm,
         scratch_shapes=returning,
         compiler_params=params(collective_id=2, has_side_effects=True),
-    )(forces_of(ext), half, source, pick)
-    return positions_end, velocities_end, forces_end
+    )(forces_of(next_ext), next_ext, names, *prepared)
+
+    return pl.pallas_call(
+        end_kernel,
+        out_shape=[atoms] * 3,
+        in_specs=[vm] * 4,
+        out_specs=[vm] * 3,
+        compiler_params=params(),
+    )(totals, half, source, pick)
 
 
 def solution(mesh):

time: 64.8 us -> 54.6 us (0.84)
  Pallas kernels: 58.6 us -> 51.9 us
  local copies, waits for them, and re-layouts: 4.53 us -> 1.06 us
    pallas_call x2, Pallas kernels: 17.6 us -> 9.06 us  [forces_of(): pl.pallas_call(pair_kernel, out_shape=lists, in_specs=[vm] * 9, out_specs...]
    unnamed x26 -> x21, local copies, waits for them, and re-layouts: 4.53 us -> 1.06 us
    pallas_call x3 -> x4, Pallas kernels: 41 us -> 42.9 us  [the longest x1 17.8 us: body(): pl.pallas_call(middle_kernel, out_shape=[lists, tile, tile], in_specs=[vm...]
where the time goes in v2:
time: 54.6 us; the launch traced here: 54.4 us
  Pallas kernels  51.9 us (95%)
  between operations  1.47 us (3%)
  local copies, waits for them, and re-layouts  1.06 us (2%)
    pallas_call x1, Pallas kernels, body(): pl.pallas_call(middle_kernel, out_shape=[lists, tile, tile], in_specs=[vm...  17.8 us
    pallas_call x1, Pallas kernels, body(): pl.pallas_call(first, out_shape=out_shape, in_specs=[vm] * 11 + [pl.Block...  13.5 us
    pallas_call x1, Pallas kernels, body(): pl.pallas_call(last_kernel, out_shape=jax.ShapeDtypeStruct((2, 8, 128), F...  10.8 us
    pallas_call x2, Pallas kernels, forces_of(): pl.pallas_call(pair_kernel, out_shape=lists, in_specs=[vm] * 9, out_specs...  9.06 us

profile of v2, /device:TPU:1, one launch (start us, length us, event | category | flops | bytes accessed | tf_op | source)
XLA Modules:
  0.0 54.4 jit_solution(14528068947236893215)
XLA Ops:
  1.3 0.0 copy-start
  1.3 0.0 copy-start.1
  1.3 0.0 copy-start.2
  1.3 0.0 copy-start.3
  1.3 0.0 copy-start.4
  1.3 0.0 copy-start.5
  1.3 0.0 copy-start.6
  1.4 0.0 copy-start.7
  1.4 0.0 copy-start.8
  1.4 0.0 copy-start.9
  1.4 1.0 %copy.16.refs_10_ = bf16[1,512,64]{2,1,0:T(8,128)(2,1)S(1)} copy(bf16[1,512,64]{1,2,0:T(8,128)(2,1)} %param.23) | data formatting | bytes 131072 | tf_op args[10]
  2.4 0.0 copy-done
  2.4 0.0 copy-done.1
  2.4 0.0 copy-done.2
  2.4 0.0 copy-done.3
  2.4 0.0 copy-done.4
  2.5 0.0 copy-done.5
  2.5 0.0 copy-done.6
  2.5 0.0 copy-done.7
  2.5 0.0 copy-done.8
  2.5 0.0 copy-done.9
  2.5 13.5 %shard_map.148 = (f32[4,8,256]{2,1,0:T(8,128)S(1)}, s32[192,128]{1,0:T(8,128)S(1)}, f32[8,128]{1,0:T(8,128)S(1)}, f32[8,128]{1,0:T(8,128)S(1)}, s32[8,128]{1,0:T...) custom-call(f32[3,48]{1,0:T(4,128)S(1)} %copy-done.4, ...), custom_call_target="tpu_custom_call" | custom-call | tf_op jit(solution)/shard_map/pallas_call | solution.py:495
  16.0 4.4 %shard_map.149.f_ref = f32[4,8,256]{2,1,0:T(8,128)S(1)} custom-call(f32[4,8,256]{2,1,0:T(8,128)S(1)} %get-tuple-element.18.ext_ref.rest_0_, s32[192,128]{1,0:T(8,128)S(1)} %get-tuple-element.19.nb_ref.rest_1_, bf16[512,32]{1,0:T(8,128)(2,1)S(1)} %get-tuple-element.20.w1_ref.rest_2_, bf16[576,512]{1,0:T(8,128)(2,1)S(1)} %get-tuple-element.21.lt_ref.rest_3_, ...), custom_call_target="tpu_custom_call" | custom-call | tf_op jit(solution)/shard_map/pallas_call | solution.py:505
  20.4 17.8 %shard_map.150 = (f32[4,8,256]{2,1,0:T(8,128)S(1)}, f32[8,128]{1,0:T(8,128)S(1)}, f32[8,128]{1,0:T(8,128)S(1)}) custom-call(f32[4,8,256]{2,1,0:T(8,128)S(1)} %shard_map.149.f_ref, f32[8,128]{1,0:T(8,128)S(1)} %get-tuple-element.27.half_ref, f32[8,128]{1,0:T(8,128)S(1)} %get-tuple-element.28.source_ref, s32[8,128]{1,0:T(8,128)S(1)} %get-tuple-element.29.pick_ref, ...), custom_call_target="tpu_custom_call" | custom-call | tf_op jit(solution)/shard_map/pallas_call | solution.py:515
  38.3 4.6 %shard_map.151.f_ref = f32[4,8,256]{2,1,0:T(8,128)S(1)} custom-call(f32[4,8,256]{2,1,0:T(8,128)S(1)} %get-tuple-element.30.ext_ref.rest_0_, s32[192,128]{1,0:T(8,128)S(1)} %get-tuple-element.19.nb_ref.rest_1_, bf16[512,32]{1,0:T(8,128)(2,1)S(1)} %get-tuple-element.20.w1_ref.rest_2_, bf16[576,512]{1,0:T(8,128)(2,1)S(1)} %get-tuple-element.21.lt_ref.rest_3_, ...), custom_call_target="tpu_custom_call" | custom-call | tf_op jit(solution)/shard_map/pallas_call | solution.py:505
  42.9 10.8 %shard_map.152.total_ref = f32[2,8,128]{2,1,0:T(8,128)S(1)} custom-call(f32[4,8,256]{2,1,0:T(8,128)S(1)} %shard_map.151.f_ref, f32[4,8,256]{2,1,0:T(8,128)S(1)} %get-tuple-element.30.ext_ref.rest_0_, s32[192,128]{1,0:T(8,128)S(1)} %get-tuple-element.19.nb_ref.rest_1_, bf16[512,32]{1,0:T(8,128)(2,1)S(1)} %get-tuple-element.20.w1_ref.rest_2_, ...), custom_call_target="tpu_custom_call" | custom-call | tf_op jit(solution)/shard_map/pallas_call | solution.py:524
  53.7 0.7 %shard_map.153 = (f32[3,48]{1,0:T(4,128)}, f32[3,48]{1,0:T(4,128)}, f32[3,48]{1,0:T(4,128)}) custom-call(f32[2,8,128]{2,1,0:T(8,128)S(1)} %shard_map.152.total_ref, f32[8,128]{1,0:T(8,128)S(1)} %get-tuple-element.31.half_ref, f32[8,128]{1,0:T(8,128)S(1)} %get-tuple-element.32.source_ref, s32[8,128]{1,0:T(8,128)S(1)} %get-tuple-element.29.pick_ref), custom_call_target="tpu_custom_call" | custom-call | tf_op jit(solution)/shard_map/pallas_call | solution.py:533
Async XLA Ops:
  1.3 1.1 %copy-start = (s32[48,128]{1,0:T(8,128)S(1)}, s32[48,128]{1,0:T(8,128)}, u32[]{:S(2)}) copy-start(s32[48,128]{1,0:T(8,128)} %refs_6_.1) | copy-start | bytes 73732
  1.3 1.1 %copy-start.1 = (bf16[2,8,512]{2,1,0:T(8,128)(2,1)S(1)}, bf16[2,8,512]{2,1,0:T(8,128)(2,1)}, u32[]{:S(2)}) copy-start(bf16[2,8,512]{2,1,0:T(8,128)(2,1)} %refs_9_.1) | copy-start | bytes 49156
  1.3 1.1 %copy-start.2 = (bf16[8,512]{1,0:T(8,128)(2,1)S(1)}, bf16[8,512]{1,0:T(8,128)(2,1)}, u32[]{:S(2)}) copy-start(bf16[8,512]{1,0:T(8,128)(2,1)} %refs_8_.1) | copy-start | bytes 24580
  1.3 1.1 %copy-start.3 = (s32[8,12]{1,0:T(8,128)S(1)}, s32[8,12]{1,0:T(8,128)}, u32[]{:S(2)}) copy-start(s32[8,12]{1,0:T(8,128)} %refs_5_.1) | copy-start | bytes 1156
  1.3 1.1 %copy-start.4 = (f32[3,48]{1,0:T(4,128)S(1)}, f32[3,48]{1,0:T(4,128)}, u32[]{:S(2)}) copy-start(f32[3,48]{1,0:T(4,128)} %refs_0_.1) | copy-start | bytes 1732
  1.3 1.1 %copy-start.5 = (f32[3,48]{1,0:T(4,128)S(1)}, f32[3,48]{1,0:T(4,128)}, u32[]{:S(2)}) copy-start(f32[3,48]{1,0:T(4,128)} %refs_1_.1) | copy-start | bytes 1732
  1.3 1.1 %copy-start.6 = (f32[3,48]{1,0:T(4,128)S(1)}, f32[3,48]{1,0:T(4,128)}, u32[]{:S(2)}) copy-start(f32[3,48]{1,0:T(4,128)} %refs_2_.1) | copy-start | bytes 1732
  1.4 1.1 %copy-start.7 = (bf16[512]{0:T(512)(128)(2,1)S(1)}, bf16[512]{0:T(512)(128)(2,1)}, u32[]{:S(2)}) copy-start(bf16[512]{0:T(512)(128)(2,1)} %refs_12_.1) | copy-start | bytes 3076
  1.4 1.1 %copy-start.8 = (s32[48]{0:T(128)S(1)}, s32[48]{0:T(128)}, u32[]{:S(2)}) copy-start(s32[48]{0:T(128)} %param.16) | copy-start | bytes 580
  1.4 1.1 %copy-start.9 = (s32[48]{0:T(128)S(1)}, s32[48]{0:T(128)}, u32[]{:S(2)}) copy-start(s32[48]{0:T(128)} %param.20) | copy-start | bytes 580

commit v3 on v2

--- a/solution.py
+++ b/solution.py
@@ -22,8 +22,9 @@
 LATENT = 512
 FEATURES = 64
 SCALE = 4.0 / SLOTS**0.5
-CHAINS = 6
-SURE = 12
+CHAINS = 8
+LAST = 3
+SURE = 14
 
 
 def mm(a, b):
@@ -67,6 +68,12 @@
 
 def greeted():
     pl.semaphore_wait(pltpu.get_barrier_semaphore(), 3 * N_YZ - 1)
+
+
+def wide_partners():
+    g, q, n = lax.axis_index("gx"), lax.axis_index("yz"), lax.axis_size("gx")
+    column = [lax.rem(q + s, N_YZ) for s in range(N_YZ)]
+    return [[(s, lax.rem(g + n + step, n), column[s]) for s in range(step == 0, N_YZ)] for step in (0, 1, -1, 2, -2)]
 
 
 def send(src, dst, sems, at, g, q):
@@ -107,22 +114,44 @@
         ext_ref[d, :, 128:256] = jnp.where(lane < 36, hi, jnp.where(lane < 72, lo, 0.0))
 
 
-def fold(f_ref, out0, out1):
+def fold(f_ref):
     lane = lanes_of((8, 128))
+    first = (lane < 12) | ((lane >= 36) & (lane < 48))
+    second = (lane < 24) | ((lane >= 48) & (lane < 60))
+    tiles = []
     for d in range(N_YZ):
         up, down = (d + 1) % N_YZ, (d - 1) % N_YZ
-        out0[d] = jnp.where(
+        tile0 = jnp.where(
             lane < ATOMS,
             f_ref[d, :, 0:128],
             jnp.where(lane < ATOMS + GHOSTS, f_ref[down, :, 0:128], f_ref[up, :, 0:128]),
         )
-        first = (lane < 12) | ((lane >= 36) & (lane < 48))
-        second = (lane < 24) | ((lane >= 48) & (lane < 60))
-        out1[d] = jnp.where(
+        tile1 = jnp.where(
             first,
             f_ref[down, :, 128:256],
             jnp.where(second, f_ref[d, :, 128:256], f_ref[up, :, 128:256]),
         )
+        tiles.append((tile0, tile1))
+    return tiles
+
+
+def pack(tiles):
+    low = jnp.where(lanes_of((8, 128)) < 64, tiles[0], pltpu.roll(tiles[1], 64, 1))
+    high = jnp.where(lanes_of((8, 128)) < 64, tiles[2], pltpu.roll(tiles[3], 64, 1))
+    return jnp.where(rows_of((8, 128)) < 4, low, pltpu.roll(high, 4, 0))
+
+
+def unpack(tile, d):
+    tile = pltpu.roll(tile, 64, 1) if d % 2 else tile
+    return pltpu.roll(tile, 4, 0) if d >= 2 else tile
+
+
+def dense(tile, picks):
+    hi = tile.astype(BF16)
+    parts = jnp.concatenate([hi.astype(F32), tile - hi.astype(F32)], axis=0).astype(BF16)
+    hot = jnp.where(rows_of((64, 128)) == picks.astype(I32), 1.0, 0.0).astype(BF16)
+    out = lax.dot_general(parts, hot, NT, preferred_element_type=F32)
+    return out[0:8] + out[8:16]
 
 
 def three(x):
@@ -151,13 +180,18 @@
     return (parts[0:8] + parts[8:16]) + parts[16:24]
 
 
-def payload(source, pick_ref):
-    return gather(source, pick_ref[0:1, :]), gather(source, pick_ref[1:2, :])
+def lists_from(ext_ref, near, near_picks, low, low_picks, high, high_picks):
+    assemble(
+        ext_ref,
+        [gather(near[d], near_picks[d][4:5].astype(I32)) for d in range(N_YZ)],
+        [gather(low[d], low_picks[d][5:6].astype(I32)) for d in range(N_YZ)],
+        [gather(high[d], high_picks[d][5:6].astype(I32)) for d in range(N_YZ)],
+    )
 
 
 def first_kernel(
     in_refs,
-    ext_ref, nball_ref, half_ref, source_ref, pick_ref, w1_ref, lt_ref, li_ref, bw_ref, ew_ref, rad_ref, rc_ref,
+    ext_ref, nball_ref, state_ref, picks_ref, pick_ref, w1_ref, lt_ref, li_ref, bw_ref, ew_ref, rad_ref, rc_ref,
     wide, sends, mine, near, low, high, nbs, sems, nbsems, latent, landed,
 ):
     greet()
@@ -180,8 +214,6 @@
     moved = wide[0] + STEP * half
     live = jnp.broadcast_to(live_ref[...].astype(F32), (8, 128))
     source = jnp.where(row < 3, moved, jnp.where(row == 3, kinds, live))
-    half_ref[...] = half
-    source_ref[...] = source
 
     sends[...] = jnp.zeros_like(sends)
     sends[:, 0:GHOSTS] = send_ref[...]
@@ -196,11 +228,9 @@
         else:
             pick1 = jnp.where(here, names, pick1)
     pick_ref[...] = jnp.where(row == 0, pick0, pick1)
-    tile0, tile1 = payload(source, pick_ref)
-    tile0 = jnp.where(row == 4, live, tile0)
-    mine[0] = tile0
-    mine[1] = tile1
-    near[me] = tile0
+    mine[0] = source
+    mine[1] = jnp.where(row < 3, half, jnp.where(row == 4, pick0.astype(F32), jnp.where(row == 5, pick1.astype(F32), live)))
+    near[me] = mine[...]
 
     diagonal = rows_of((ATOMS, ATOMS)) == lanes_of((ATOMS, ATOMS))
     counts = jnp.sum(jnp.where(diagonal, count_ref[...].astype(F32), 0.0), axis=1, keepdims=True)
@@ -215,16 +245,25 @@
     nbs[me] = jnp.where(used, names, -1)
 
     greeted()
-    copies = spread(lambda q: (mine.at[0], mine.at[1]), near, low, high, sems)
-    for s, g, q in slab:
-        copies.append(send(nbs.at[me], nbs.at[me], nbsems, s - 1, g, q))
+    copies = spread(lambda q: (mine, mine), near, low, high, sems)
+    names = [send(nbs.at[me], nbs.at[me], nbsems, s - 1, g, q) for s, g, q in slab]
 
     load.wait()
     prepare(radial_ref, embed_ref, env_ref, latent, read_ref, w1_ref, lt_ref, li_ref, bw_ref, ew_ref, rad_ref, rc_ref)
 
     for copy in copies:
         copy.wait()
-    assemble(ext_ref, near, low, high)
+    slabs = [[(buffer[d, 0], buffer[d, 1]) for d in range(N_YZ)] for buffer in (low, near, high)]
+    places = [[one[0] for one in slab] for slab in slabs]
+    others = [[one[1] for one in slab] for slab in slabs]
+    lists_from(ext_ref, places[1], others[1], places[0], others[0], places[2], others[2])
+    for i in range(3):
+        state_ref[i] = pack(places[i])
+        state_ref[3 + i] = pack(others[i])
+        for d in range(N_YZ):
+            picks_ref[i, d] = others[i][d]
+    for copy in names:
+        copy.wait()
     for d in range(N_YZ):
         nball_ref[d * ATOMS : (d + 1) * ATOMS, :] = nbs[d]
 
@@ -252,46 +291,90 @@
     rc_ref[...] = column
 
 
-def collect(f_ref, refs, fsum, own, back0, back1, near, low, high, sems):
+def middle_kernel(
+    f_ref, state_ref, picks_ref, *rest
+):
+    refs, (next_ext_ref, half_two_ref, next_ref), scratch = rest[:9], rest[9:12], rest[12:]
+    fsum, own, message, slab_in, up_in, down_in, up2_in, down2_in, sems = scratch
+    me = lax.axis_index("yz")
+    row = rows_of((8, 128))
+    lane = lanes_of((8, 128))
+    slab, above, below, above2, below2 = wide_partners()
+    barrier = pltpu.get_barrier_semaphore()
+    for _, g, q in slab + above + below + above2 + below2:
+        pl.semaphore_signal(barrier, inc=1, device_id=(g, q), device_id_type=MESH)
+    sure_forces(fsum, own, f_ref, refs)
+    found = [[], [], []]
+    for d, (tile0, tile1) in enumerate(fold(fsum)):
+        tile0 = jnp.where(lane < NEAR, tile0, 0.0)
+        ours, theirs = jnp.where(lane < 36, tile1, 0.0), jnp.where((lane >= 36) & (lane < 72), tile1, 0.0)
+        found[0].append(dense(theirs, picks_ref[0, d, 5:6, :]))
+        found[1].append(dense(tile0, picks_ref[1, d, 4:5, :]))
+        found[2].append(dense(ours, picks_ref[2, d, 5:6, :]))
+    for i in range(3):
+        first = jnp.concatenate(found[i][0:2], axis=1)
+        second = jnp.concatenate(found[i][2:4], axis=1)
+        message[i] = jnp.where(row < 4, first, pltpu.roll(second, 4, 0))
+    slab_in[me] = message[...]
+    pl.semaphore_wait(barrier, 5 * N_YZ - 1)
+    copies = []
+    at = 0
+    for group, part, buffer in (
+        (above2, message.at[2:3], down2_in), (below2, message.at[0:1], up2_in), (above, message.at[1:3], down_in),
+        (below, message.at[0:2], up_in), (slab, message, slab_in),
+    ):
+        for _, g, q in group:
+            copies.append(send(part, buffer.at[me], sems, at, g, q))
+            at += 1
+    factors = []
+    for i in range(3):
+        place = state_ref[i]
+        factors.append(0.5 * STEP * inverse_mass(jnp.where(row < 4, place[3:4], place[7:8])))
+    for copy in copies:
+        copy.wait()
+
+    def over(pick):
+        return (pick(0) + pick(1)) + (pick(2) + pick(3))
+
+    forces = [
+        over(lambda q: slab_in[q, 0]) + over(lambda q: down_in[q, 0]) + over(lambda q: down2_in[q, 0]),
+        over(lambda q: slab_in[q, 1]) + over(lambda q: up_in[q, 0]) + over(lambda q: down_in[q, 1]),
+        over(lambda q: slab_in[q, 2]) + over(lambda q: up_in[q, 1]) + over(lambda q: up2_in[q, 0]),
+    ]
+    coordinate = (row != 3) & (row != 7)
+    places = []
+    for i in range(3):
+        place = state_ref[i]
+        kick = factors[i] * forces[i]
+        half_two = (state_ref[3 + i] + kick) + kick
+        place = jnp.where(coordinate, place + STEP * half_two, place)
+        tiles = [jnp.where(row == 4, picks_ref[i, d, 6:7, :], unpack(place, d)) for d in range(N_YZ)]
+        places.append(tiles)
+        if i == 1:
+            own_half, own_place = unpack(half_two, 0), tiles[0]
+            for d in range(1, N_YZ):
+                own_half = jnp.where(me == d, unpack(half_two, d), own_half)
+                own_place = jnp.where(me == d, tiles[d], own_place)
+            half_two_ref[...] = own_half
+            next_ref[...] = own_place
+    picks = [[picks_ref[i, d] for d in range(N_YZ)] for i in range(3)]
+    lists_from(next_ext_ref, places[1], picks[1], places[0], picks[0], places[2], picks[2])
+
+
+def last_kernel(f_ref, *rest):
+    refs, total_ref, scratch = rest[:9], rest[9], rest[10:]
+    fsum, own, back0, back1, near, low, high, sems = scratch
     me = lax.axis_index("yz")
     greet()
     sure_forces(fsum, own, f_ref, refs)
-    fold(fsum, back0, back1)
+    for d, (tile0, tile1) in enumerate(fold(fsum)):
+        back0[d] = tile0
+        back1[d] = tile1
     near[me] = back0[me]
     greeted()
     for copy in spread(lambda q: (back0.at[q], back1.at[q]), near, low, high, sems):
         copy.wait()
-    return gathered(near, low, high)
-
-
-def middle_kernel(
-    f_ref, half_ref, source_ref, pick_ref, *rest
-):
-    refs, (next_ext_ref, half_two_ref, next_ref), scratch = rest[:9], rest[9:12], rest[12:]
-    mine, near, low, high, sems = scratch[8:]
-    me = lax.axis_index("yz")
-    row = rows_of((8, 128))
-    forces = own_forces(*collect(f_ref, refs, *scratch[:8]), pick_ref)
-    source = source_ref[...]
-    kick = 0.5 * STEP * inverse_mass(jnp.broadcast_to(source[3:4], (8, 128))) * forces
-    half_two = (half_ref[...] + kick) + kick
-    source = jnp.where(row < 3, source + STEP * half_two, source)
-    tile0, tile1 = payload(source, pick_ref)
-    tile0 = jnp.where(row == 4, jnp.broadcast_to(source[4:5], (8, 128)), tile0)
-    mine[0] = tile0
-    mine[1] = tile1
-    near[me] = tile0
-    copies = spread(lambda q: (mine.at[0], mine.at[1]), near, low, high, sems)
-    half_two_ref[...] = half_two
-    next_ref[...] = source
-    for copy in copies:
-        copy.wait()
-    assemble(next_ext_ref, near, low, high)
-
-
-def last_kernel(f_ref, *rest):
-    refs, total_ref, scratch = rest[:9], rest[9], rest[10:]
-    total_ref[0], total_ref[1] = collect(f_ref, refs, *scratch)
+    total_ref[0], total_ref[1] = gathered(near, low, high)
 
 
 def end_kernel(total_ref, half_ref, source_ref, pick_ref, pos_ref, vel_ref, force_ref):
@@ -405,12 +488,14 @@
     ends = []
     total = jnp.int32(0)
     for d in range(N_YZ):
-        total = total + jnp.max(ext_ref[d, 4:5, 0:1]).astype(I32) - SURE
+        total = total + lax.max(jnp.max(ext_ref[d, 4:5, 0:1]).astype(I32) - SURE, 0)
         ends.append(total)
     me = lax.axis_index("yz")
     first = (total * me) // N_YZ
     last = (total * (me + 1)) // N_YZ
-    steps = lax.max(last - first + CHAINS - 1, 0) // (2 * CHAINS)
+    count = last - first
+    step_size = 2 * CHAINS
+    steps = lax.max(count - 2 * LAST + step_size - 1, 0) // step_size
 
     def add(domain, value):
         sums[domain, :, 0:EXT] += value
@@ -436,11 +521,11 @@
         return carry
 
     lax.fori_loop(0, steps, step, 0)
-    rest = first + steps * 2 * CHAINS
-
-    @pl.when(rest < last)
+    start = first + steps * step_size
+
+    @pl.when(start < last)
     def _():
-        work(rest, CHAINS // 2)
+        work(start, LAST)
 
     for d in range(N_YZ):
         f_ref[d, :, 0:128], f_ref[d, :, 128:256] = split(sums[d, :, 0:128], sums[d, :, 128:256])
@@ -481,10 +566,11 @@
         readout,
     )
     weights = [(LATENT, 32), (FEATURES + LATENT, LATENT), (LATENT, FEATURES), (FEATURES + LATENT, LATENT), (LATENT, FEATURES + 16), (16, LATENT)]
-    out_shape = [lists, jax.ShapeDtypeStruct((N_YZ * ATOMS, SLOTS), I32), tile, tile, jax.ShapeDtypeStruct((8, 128), I32)]
+    out_shape = [lists, jax.ShapeDtypeStruct((N_YZ * ATOMS, SLOTS), I32), jax.ShapeDtypeStruct((6, 8, 128), F32)]
+    out_shape += [jax.ShapeDtypeStruct((3, N_YZ, 8, 128), F32), jax.ShapeDtypeStruct((8, 128), I32)]
     out_shape += [jax.ShapeDtypeStruct(s, BF16) for s in weights] + [jax.ShapeDtypeStruct((LATENT, 128), F32)]
     scratch = [
-        pltpu.VMEM((4, 8, 128), F32), pltpu.VMEM((8, 128), I32), pltpu.VMEM((2, 8, 128), F32), four, four, four,
+        pltpu.VMEM((4, 8, 128), F32), pltpu.VMEM((8, 128), I32), pltpu.VMEM((2, 8, 128), F32), *[pltpu.VMEM((N_YZ, 2, 8, 128), F32)] * 3,
         pltpu.VMEM((N_YZ, ATOMS, SLOTS), I32), copies, pltpu.SemaphoreType.DMA((2, N_YZ - 1)),
         pltpu.VMEM(latent_weight.shape, BF16), pltpu.SemaphoreType.DMA,
     ]
@@ -492,7 +578,7 @@
     def first(*refs):
         first_kernel(refs[: len(args)], *refs[len(args) :])
 
-    ext, names, half, source, pick, *prepared = pl.pallas_call(
+    ext, names, state, picks, pick, *prepared = pl.pallas_call(
         first,
         out_shape=out_shape,
         in_specs=[vm] * 11 + [pl.BlockSpec(memory_space=pl.ANY), vm],
@@ -515,11 +601,13 @@
     next_ext, half, source = pl.pallas_call(
         middle_kernel,
         out_shape=[lists, tile, tile],
-        in_specs=[vm] * 13,
+        in_specs=[vm] * 12,
         out_specs=[vm] * 3,
-        scratch_shapes=returning + [pltpu.VMEM((2, 8, 128), F32), four, four, four, copies],
+        scratch_shapes=[sums, pltpu.VMEM((8, 256), F32), pltpu.VMEM((3, 8, 128), F32)]
+        + [pltpu.VMEM((N_YZ, n, 8, 128), F32) for n in (3, 2, 2, 1, 1)]
+        + [pltpu.SemaphoreType.DMA((2, 5 * N_YZ - 1))],
         compiler_params=params(collective_id=1, has_side_effects=True),
-    )(forces_of(ext), half, source, pick, ext, names, *prepared)
+    )(forces_of(ext), state, picks, ext, names, *prepared)
 
     totals = pl.pallas_call(
         last_kernel,

time: 54.6 us -> 53 us (0.971)
  Pallas kernels: 51.9 us -> 50.3 us
    pallas_call x2, Pallas kernels: 9.06 us -> 5.64 us  [forces_of(): pl.pallas_call(pair_kernel, out_shape=lists, in_specs=[vm] * 9, out_specs...]
    pallas_call x1, Pallas kernels: 10.8 us -> 12.8 us  [body(): pl.pallas_call(last_kernel, out_shape=jax.ShapeDtypeStruct((2, 8, 128), F...]
where the time goes in v3:
time: 53 us; the launch traced here: 52.8 us
  Pallas kernels  50.3 us (95%)
  between operations  1.47 us (3%)
  local copies, waits for them, and re-layouts  1.06 us (2%)
    pallas_call x1, Pallas kernels, body(): pl.pallas_call(middle_kernel, out_shape=[lists, tile, tile], in_specs=[vm...  17.4 us
    pallas_call x1, Pallas kernels, body(): pl.pallas_call(first, out_shape=out_shape, in_specs=[vm] * 11 + [pl.Block...  13.6 us
    pallas_call x1, Pallas kernels, body(): pl.pallas_call(last_kernel, out_shape=jax.ShapeDtypeStruct((2, 8, 128), F...  12.8 us
    pallas_call x2, Pallas kernels, forces_of(): pl.pallas_call(pair_kernel, out_shape=lists, in_specs=[vm] * 9, out_specs...  5.64 us

profile of v3, /device:TPU:1, one launch (start us, length us, event | category | flops | bytes accessed | tf_op | source)
XLA Modules:
  0.0 52.8 jit_solution(5183238028630769294)
XLA Ops:
  1.3 0.0 copy-start
  1.3 0.0 copy-start.1
  1.3 0.0 copy-start.2
  1.3 0.0 copy-start.3
  1.3 0.0 copy-start.4
  1.3 0.0 copy-start.5
  1.3 0.0 copy-start.6
  1.4 0.0 copy-start.7
  1.4 0.0 copy-start.8
  1.4 0.0 copy-start.9
  1.4 1.0 %copy.16.refs_10_ = bf16[1,512,64]{2,1,0:T(8,128)(2,1)S(1)} copy(bf16[1,512,64]{1,2,0:T(8,128)(2,1)} %param.23) | data formatting | bytes 131072 | tf_op args[10]
  2.4 0.0 copy-done
  2.4 0.0 copy-done.1
  2.4 0.0 copy-done.2
  2.4 0.0 copy-done.3
  2.4 0.0 copy-done.4
  2.5 0.0 copy-done.5
  2.5 0.0 copy-done.6
  2.5 0.0 copy-done.7
  2.5 0.0 copy-done.8
  2.5 0.0 copy-done.9
  2.5 13.6 %shard_map.148 = (f32[4,8,256]{2,1,0:T(8,128)S(1)}, s32[192,128]{1,0:T(8,128)S(1)}, f32[6,8,128]{2,1,0:T(8,128)S(1)}, f32[3,4,8,128]{3,2,1,0:T(8,128)S(1)}, s32[...) custom-call(f32[3,48]{1,0:T(4,128)S(1)} %copy-done.4, ...), custom_call_target="tpu_custom_call" | custom-call | tf_op jit(solution)/shard_map/pallas_call | solution.py:581
  16.1 2.8 %shard_map.149.f_ref = f32[4,8,256]{2,1,0:T(8,128)S(1)} custom-call(f32[4,8,256]{2,1,0:T(8,128)S(1)} %get-tuple-element.18.ext_ref.rest_0_, s32[192,128]{1,0:T(8,128)S(1)} %get-tuple-element.19.nb_ref.rest_1_, bf16[512,32]{1,0:T(8,128)(2,1)S(1)} %get-tuple-element.20.w1_ref.rest_2_, bf16[576,512]{1,0:T(8,128)(2,1)S(1)} %get-tuple-element.21.lt_ref.rest_3_, ...), custom_call_target="tpu_custom_call" | custom-call | tf_op jit(solution)/shard_map/pallas_call | solution.py:591
  18.9 17.4 %shard_map.150 = (f32[4,8,256]{2,1,0:T(8,128)S(1)}, f32[8,128]{1,0:T(8,128)S(1)}, f32[8,128]{1,0:T(8,128)S(1)}) custom-call(f32[4,8,256]{2,1,0:T(8,128)S(1)} %shard_map.149.f_ref, f32[6,8,128]{2,1,0:T(8,128)S(1)} %get-tuple-element.27.state_ref, f32[3,4,8,128]{3,2,1,0:T(8,128)S(1)} %get-tuple-element.28.picks_ref, ...), custom_call_target="tpu_custom_call" | custom-call | tf_op jit(solution)/shard_map/pallas_call | solution.py:601
  36.4 2.9 %shard_map.151.f_ref = f32[4,8,256]{2,1,0:T(8,128)S(1)} custom-call(f32[4,8,256]{2,1,0:T(8,128)S(1)} %get-tuple-element.29.ext_ref.rest_0_, s32[192,128]{1,0:T(8,128)S(1)} %get-tuple-element.19.nb_ref.rest_1_, bf16[512,32]{1,0:T(8,128)(2,1)S(1)} %get-tuple-element.20.w1_ref.rest_2_, bf16[576,512]{1,0:T(8,128)(2,1)S(1)} %get-tuple-element.21.lt_ref.rest_3_, ...), custom_call_target="tpu_custom_call" | custom-call | tf_op jit(solution)/shard_map/pallas_call | solution.py:591
  39.2 12.8 %shard_map.152.total_ref = f32[2,8,128]{2,1,0:T(8,128)S(1)} custom-call(f32[4,8,256]{2,1,0:T(8,128)S(1)} %shard_map.151.f_ref, f32[4,8,256]{2,1,0:T(8,128)S(1)} %get-tuple-element.29.ext_ref.rest_0_, s32[192,128]{1,0:T(8,128)S(1)} %get-tuple-element.19.nb_ref.rest_1_, bf16[512,32]{1,0:T(8,128)(2,1)S(1)} %get-tuple-element.20.w1_ref.rest_2_, ...), custom_call_target="tpu_custom_call" | custom-call | tf_op jit(solution)/shard_map/pallas_call | solution.py:612
  52.1 0.7 %shard_map.153 = (f32[3,48]{1,0:T(4,128)}, f32[3,48]{1,0:T(4,128)}, f32[3,48]{1,0:T(4,128)}) custom-call(f32[2,8,128]{2,1,0:T(8,128)S(1)} %shard_map.152.total_ref, f32[8,128]{1,0:T(8,128)S(1)} %get-tuple-element.30.half_ref, f32[8,128]{1,0:T(8,128)S(1)} %get-tuple-element.31.source_ref, s32[8,128]{1,0:T(8,128)S(1)} %get-tuple-element.32.pick_ref), custom_call_target="tpu_custom_call" | custom-call | tf_op jit(solution)/shard_map/pallas_call | solution.py:621
Async XLA Ops:
  1.3 1.1 %copy-start = (s32[48,128]{1,0:T(8,128)S(1)}, s32[48,128]{1,0:T(8,128)}, u32[]{:S(2)}) copy-start(s32[48,128]{1,0:T(8,128)} %refs_6_.1) | copy-start | bytes 73732
  1.3 1.1 %copy-start.1 = (bf16[2,8,512]{2,1,0:T(8,128)(2,1)S(1)}, bf16[2,8,512]{2,1,0:T(8,128)(2,1)}, u32[]{:S(2)}) copy-start(bf16[2,8,512]{2,1,0:T(8,128)(2,1)} %refs_9_.1) | copy-start | bytes 49156
  1.3 1.1 %copy-start.2 = (bf16[8,512]{1,0:T(8,128)(2,1)S(1)}, bf16[8,512]{1,0:T(8,128)(2,1)}, u32[]{:S(2)}) copy-start(bf16[8,512]{1,0:T(8,128)(2,1)} %refs_8_.1) | copy-start | bytes 24580
  1.3 1.1 %copy-start.3 = (s32[8,12]{1,0:T(8,128)S(1)}, s32[8,12]{1,0:T(8,128)}, u32[]{:S(2)}) copy-start(s32[8,12]{1,0:T(8,128)} %refs_5_.1) | copy-start | bytes 1156
  1.3 1.1 %copy-start.4 = (f32[3,48]{1,0:T(4,128)S(1)}, f32[3,48]{1,0:T(4,128)}, u32[]{:S(2)}) copy-start(f32[3,48]{1,0:T(4,128)} %refs_0_.1) | copy-start | bytes 1732
  1.3 1.1 %copy-start.5 = (f32[3,48]{1,0:T(4,128)S(1)}, f32[3,48]{1,0:T(4,128)}, u32[]{:S(2)}) copy-start(f32[3,48]{1,0:T(4,128)} %refs_1_.1) | copy-start | bytes 1732
  1.3 1.1 %copy-start.6 = (f32[3,48]{1,0:T(4,128)S(1)}, f32[3,48]{1,0:T(4,128)}, u32[]{:S(2)}) copy-start(f32[3,48]{1,0:T(4,128)} %refs_2_.1) | copy-start | bytes 1732
  1.4 1.1 %copy-start.7 = (bf16[512]{0:T(512)(128)(2,1)S(1)}, bf16[512]{0:T(512)(128)(2,1)}, u32[]{:S(2)}) copy-start(bf16[512]{0:T(512)(128)(2,1)} %refs_12_.1) | copy-start | bytes 3076
  1.4 1.1 %copy-start.8 = (s32[48]{0:T(128)S(1)}, s32[48]{0:T(128)}, u32[]{:S(2)}) copy-start(s32[48]{0:T(128)} %param.16) | copy-start | bytes 580
  1.4 1.1 %copy-start.9 = (s32[48]{0:T(128)S(1)}, s32[48]{0:T(128)}, u32[]{:S(2)}) copy-start(s32[48]{0:T(128)} %param.20) | copy-start | bytes 580

commit v4 on v3

--- a/solution.py
+++ b/solution.py
@@ -22,9 +22,9 @@
 LATENT = 512
 FEATURES = 64
 SCALE = 4.0 / SLOTS**0.5
-CHAINS = 8
+CHAINS = 6
 LAST = 3
-SURE = 14
+SURE = 12
 
 
 def mm(a, b):
@@ -408,13 +408,13 @@
         own = jnp.where(kind == centre[3:4], 1.0, 0.0)
         inputs.append(jnp.concatenate([basis, theirs, own, jnp.zeros((8, 128), F32)], axis=0).astype(BF16))
         geo.append((names, u, inside, env, basis * delta))
-    hp = mm(w1_ref[...], jnp.concatenate(inputs, axis=1)).astype(BF16)
+    hp = mm(w1_ref[...], jnp.concatenate(inputs, axis=1))
     yield
     y1 = 1.0 + jnp.tanh(hp)
     h0 = hp * y1
     d1 = y1 + h0 * (2.0 - y1)
     yield
-    zv = mm(lt_ref[...], h0)
+    zv = mm(lt_ref[...], h0.astype(BF16))
     yield
     inner, kept = [], []
     for c, (names, u, inside, env, slope) in enumerate(geo):
@@ -425,15 +425,15 @@
         inner.append((z * q).astype(BF16))
         kept.append((z, ue, c4, q))
     yield
-    vp = (zv[FEATURES:] + mm(li_ref[...], jnp.concatenate(inner, axis=1))).astype(BF16)
+    vp = zv[FEATURES:] + mm(li_ref[...], jnp.concatenate(inner, axis=1))
     yield
     y2 = 1.0 + jnp.tanh(vp)
     s2 = vp * y2
     d2 = y2 + s2 * (2.0 - y2)
-    h2 = (h0 + s2).astype(F32)
+    h2 = h0 + s2
     p = [jnp.sum(h2[:, c * 128 : c * 128 + 128] * rc_ref[...], axis=0, keepdims=True) for c in range(len(geo))]
     yield
-    dj = mm(bw_ref[...], d2)
+    dj = mm(bw_ref[...], d2.astype(BF16))
     yield
     sums, dws = [], []
     for c, (names, u, inside, env, slope) in enumerate(geo):
@@ -450,7 +450,7 @@
     yield
     a = dj[FEATURES:] + mm(ew_ref[...], dw)
     yield
-    db = mm(rad_ref[...], a.astype(BF16) * d1)
+    db = mm(rad_ref[...], (a * d1).astype(BF16))
     yield
     for c, (names, u, inside, env, slope) in enumerate(geo):
         domain, slot, active = items[c]

time: 53 us -> 50.8 us (0.958); the launches traced: 52.8 us -> 51.6 us
  Pallas kernels: 50.3 us -> 49 us
    pallas_call x1, Pallas kernels: 12.8 us -> 12 us  [body(): pl.pallas_call(last_kernel, out_shape=jax.ShapeDtypeStruct((2, 8, 128), F...]
    pallas_call x1, Pallas kernels: 17.4 us -> 16.7 us  [body(): pl.pallas_call(middle_kernel, out_shape=[lists, tile, tile], in_specs=[vm...]
where the time goes in v4:
time: 50.8 us; the launch traced here: 51.6 us
  Pallas kernels  49 us (96%)
  between operations  1.47 us (3%)
  local copies, waits for them, and re-layouts  1.06 us (2%)
    pallas_call x1, Pallas kernels, body(): pl.pallas_call(middle_kernel, out_shape=[lists, tile, tile], in_specs=[vm...  16.7 us
    pallas_call x1, Pallas kernels, body(): pl.pallas_call(first, out_shape=out_shape, in_specs=[vm] * 11 + [pl.Block...  13.6 us
    pallas_call x1, Pallas kernels, body(): pl.pallas_call(last_kernel, out_shape=jax.ShapeDtypeStruct((2, 8, 128), F...  12 us
    pallas_call x2, Pallas kernels, forces_of(): pl.pallas_call(pair_kernel, out_shape=lists, in_specs=[vm] * 9, out_specs...  6.01 us
    unnamed x21, local copies, waits for them, and re-layouts  1.06 us

profile of v4, /device:TPU:1, one launch (start us, length us, event | category | flops | bytes accessed | tf_op | source)
XLA Modules:
  0.0 51.6 jit_solution(1200488013779587514)
XLA Ops:
  1.3 0.0 copy-start
  1.3 0.0 copy-start.1
  1.3 0.0 copy-start.2
  1.3 0.0 copy-start.3
  1.3 0.0 copy-start.4
  1.3 0.0 copy-start.5
  1.3 0.0 copy-start.6
  1.4 0.0 copy-start.7
  1.4 0.0 copy-start.8
  1.4 0.0 copy-start.9
  1.4 1.0 %copy.16.refs_10_ = bf16[1,512,64]{2,1,0:T(8,128)(2,1)S(1)} copy(bf16[1,512,64]{1,2,0:T(8,128)(2,1)} %param.23) | data formatting | bytes 131072 | tf_op args[10]
  2.4 0.0 copy-done
  2.4 0.0 copy-done.1
  2.4 0.0 copy-done.2
  2.4 0.0 copy-done.3
  2.4 0.0 copy-done.4
  2.5 0.0 copy-done.5
  2.5 0.0 copy-done.6
  2.5 0.0 copy-done.7
  2.5 0.0 copy-done.8
  2.5 0.0 copy-done.9
  2.5 13.6 %shard_map.148 = (f32[4,8,256]{2,1,0:T(8,128)S(1)}, s32[192,128]{1,0:T(8,128)S(1)}, f32[6,8,128]{2,1,0:T(8,128)S(1)}, f32[3,4,8,128]{3,2,1,0:T(8,128)S(1)}, s32[...) custom-call(f32[3,48]{1,0:T(4,128)S(1)} %copy-done.4, ...), custom_call_target="tpu_custom_call" | custom-call | tf_op jit(solution)/shard_map/pallas_call | solution.py:581
  16.1 3.0 %shard_map.149.f_ref = f32[4,8,256]{2,1,0:T(8,128)S(1)} custom-call(f32[4,8,256]{2,1,0:T(8,128)S(1)} %get-tuple-element.18.ext_ref.rest_0_, s32[192,128]{1,0:T(8,128)S(1)} %get-tuple-element.19.nb_ref.rest_1_, bf16[512,32]{1,0:T(8,128)(2,1)S(1)} %get-tuple-element.20.w1_ref.rest_2_, bf16[576,512]{1,0:T(8,128)(2,1)S(1)} %get-tuple-element.21.lt_ref.rest_3_, ...), custom_call_target="tpu_custom_call" | custom-call | tf_op jit(solution)/shard_map/pallas_call | solution.py:591
  19.1 16.7 %shard_map.150 = (f32[4,8,256]{2,1,0:T(8,128)S(1)}, f32[8,128]{1,0:T(8,128)S(1)}, f32[8,128]{1,0:T(8,128)S(1)}) custom-call(f32[4,8,256]{2,1,0:T(8,128)S(1)} %shard_map.149.f_ref, f32[6,8,128]{2,1,0:T(8,128)S(1)} %get-tuple-element.27.state_ref, f32[3,4,8,128]{3,2,1,0:T(8,128)S(1)} %get-tuple-element.28.picks_ref, ...), custom_call_target="tpu_custom_call" | custom-call | tf_op jit(solution)/shard_map/pallas_call | solution.py:601
  35.8 3.0 %shard_map.151.f_ref = f32[4,8,256]{2,1,0:T(8,128)S(1)} custom-call(f32[4,8,256]{2,1,0:T(8,128)S(1)} %get-tuple-element.29.ext_ref.rest_0_, s32[192,128]{1,0:T(8,128)S(1)} %get-tuple-element.19.nb_ref.rest_1_, bf16[512,32]{1,0:T(8,128)(2,1)S(1)} %get-tuple-element.20.w1_ref.rest_2_, bf16[576,512]{1,0:T(8,128)(2,1)S(1)} %get-tuple-element.21.lt_ref.rest_3_, ...), custom_call_target="tpu_custom_call" | custom-call | tf_op jit(solution)/shard_map/pallas_call | solution.py:591
  38.8 12.0 %shard_map.152.total_ref = f32[2,8,128]{2,1,0:T(8,128)S(1)} custom-call(f32[4,8,256]{2,1,0:T(8,128)S(1)} %shard_map.151.f_ref, f32[4,8,256]{2,1,0:T(8,128)S(1)} %get-tuple-element.29.ext_ref.rest_0_, s32[192,128]{1,0:T(8,128)S(1)} %get-tuple-element.19.nb_ref.rest_1_, bf16[512,32]{1,0:T(8,128)(2,1)S(1)} %get-tuple-element.20.w1_ref.rest_2_, ...), custom_call_target="tpu_custom_call" | custom-call | tf_op jit(solution)/shard_map/pallas_call | solution.py:612
  50.8 0.7 %shard_map.153 = (f32[3,48]{1,0:T(4,128)}, f32[3,48]{1,0:T(4,128)}, f32[3,48]{1,0:T(4,128)}) custom-call(f32[2,8,128]{2,1,0:T(8,128)S(1)} %shard_map.152.total_ref, f32[8,128]{1,0:T(8,128)S(1)} %get-tuple-element.30.half_ref, f32[8,128]{1,0:T(8,128)S(1)} %get-tuple-element.31.source_ref, s32[8,128]{1,0:T(8,128)S(1)} %get-tuple-element.32.pick_ref), custom_call_target="tpu_custom_call" | custom-call | tf_op jit(solution)/shard_map/pallas_call | solution.py:621
Async XLA Ops:
  1.3 1.1 %copy-start = (s32[48,128]{1,0:T(8,128)S(1)}, s32[48,128]{1,0:T(8,128)}, u32[]{:S(2)}) copy-start(s32[48,128]{1,0:T(8,128)} %refs_6_.1) | copy-start | bytes 73732
  1.3 1.1 %copy-start.1 = (bf16[2,8,512]{2,1,0:T(8,128)(2,1)S(1)}, bf16[2,8,512]{2,1,0:T(8,128)(2,1)}, u32[]{:S(2)}) copy-start(bf16[2,8,512]{2,1,0:T(8,128)(2,1)} %refs_9_.1) | copy-start | bytes 49156
  1.3 1.1 %copy-start.2 = (bf16[8,512]{1,0:T(8,128)(2,1)S(1)}, bf16[8,512]{1,0:T(8,128)(2,1)}, u32[]{:S(2)}) copy-start(bf16[8,512]{1,0:T(8,128)(2,1)} %refs_8_.1) | copy-start | bytes 24580
  1.3 1.1 %copy-start.3 = (s32[8,12]{1,0:T(8,128)S(1)}, s32[8,12]{1,0:T(8,128)}, u32[]{:S(2)}) copy-start(s32[8,12]{1,0:T(8,128)} %refs_5_.1) | copy-start | bytes 1156
  1.3 1.1 %copy-start.4 = (f32[3,48]{1,0:T(4,128)S(1)}, f32[3,48]{1,0:T(4,128)}, u32[]{:S(2)}) copy-start(f32[3,48]{1,0:T(4,128)} %refs_0_.1) | copy-start | bytes 1732
  1.3 1.1 %copy-start.5 = (f32[3,48]{1,0:T(4,128)S(1)}, f32[3,48]{1,0:T(4,128)}, u32[]{:S(2)}) copy-start(f32[3,48]{1,0:T(4,128)} %refs_1_.1) | copy-start | bytes 1732
  1.3 1.1 %copy-start.6 = (f32[3,48]{1,0:T(4,128)S(1)}, f32[3,48]{1,0:T(4,128)}, u32[]{:S(2)}) copy-start(f32[3,48]{1,0:T(4,128)} %refs_2_.1) | copy-start | bytes 1732
  1.4 1.1 %copy-start.7 = (bf16[512]{0:T(512)(128)(2,1)S(1)}, bf16[512]{0:T(512)(128)(2,1)}, u32[]{:S(2)}) copy-start(bf16[512]{0:T(512)(128)(2,1)} %refs_12_.1) | copy-start | bytes 3076
  1.4 1.1 %copy-start.8 = (s32[48]{0:T(128)S(1)}, s32[48]{0:T(128)}, u32[]{:S(2)}) copy-start(s32[48]{0:T(128)} %param.16) | copy-start | bytes 580
  1.4 1.1 %copy-start.9 = (s32[48]{0:T(128)S(1)}, s32[48]{0:T(128)}, u32[]{:S(2)}) copy-start(s32[48]{0:T(128)} %param.20) | copy-start | bytes 580
